TPU v7x, 512 devices: a whole 4x8x8 slice. The times are simulated.
512 devices in a mesh: row: 32 (over y_lo, z, core), col: 16 (over y_hi, x).
Axes of the slice: x: 4, y: 8 (y_hi: 4, y_lo: 2; y = y_hi * 2 + y_lo), z: 8, core: 2. Of those that a mesh axis runs over, the one named last changes fastest.
Arguments:
- normed: bfloat16 [768, 8192], P('col', 'row'), may hold values from -6 to 6
- gate_w: bfloat16 [8192, 14336], P('row', 'col'), may hold values from -0.0625 to 0.0625
- up_w: bfloat16 [8192, 14336], P('row', 'col'), may hold values from -0.0625 to 0.0625
- down_w: bfloat16 [14336, 8192], P('col', 'row'), may hold values from -0.046875 to 0.046875
- gate_pre: bfloat16 [768, 14336], P('row', 'col'), may hold values from -8 to 8
- up_pre: bfloat16 [768, 14336], P('row', 'col'), may hold values from -6 to 6
- block_out: bfloat16 [768, 8192], P('col', 'row'), may hold values from -6 to 6
- value_w: float32 [8192], P('row'), may hold values from -2 to 2
- q_target: float32 [768], P('col'), may hold values from -10 to 10
- grad_out: bfloat16 [768, 8192], P('col', 'row'), may hold values from -6 to 6
Outputs:
- grad_normed: bfloat16 [768, 8192], P('col', 'row')
- grad_gate: bfloat16 [8192, 14336], P('row', 'col')
- grad_up: bfloat16 [8192, 14336], P('row', 'col')
- grad_down: bfloat16 [14336, 8192], P('col', 'row')
All inputs are finite; a program needn't handle non-finite values.
Results may differ from a plain program's by a relative error of at most 0.0058.
Values may be sent and summed in bfloat16 or wider, within the bound.
A program may use at most 64 MiB of HBM per device.

v0:
```python
import jax
import jax.numpy as jnp
from jax import lax
from jax.sharding import PartitionSpec as P

expectile = 0.7
value_scale = 8.0


def output_grad(value_w, q_target, grad_out, value_est):
    margin = q_target - value_est
    weighting = jnp.where(margin > 0, expectile, 1.0 - expectile)
    value_grad = -2.0 * value_scale * weighting * margin
    return (grad_out.astype(jnp.float32) + value_grad[:, None] * value_w[None, :]).astype(
        jnp.bfloat16
    )


def swiglu_back(hidden_grad, gate_pre, up_pre):
    gate_val = gate_pre.astype(jnp.float32)
    up_val = up_pre.astype(jnp.float32)
    sigmoid_val = jax.nn.sigmoid(gate_val)
    silu_val = gate_val * sigmoid_val
    act_out = (silu_val * up_val).astype(jnp.bfloat16)
    gate_back = (
        hidden_grad * up_val * sigmoid_val * (1.0 + gate_val * (1.0 - sigmoid_val))
    ).astype(jnp.bfloat16)
    up_back = (hidden_grad * silu_val).astype(jnp.bfloat16)
    return (gate_back, up_back, act_out)


def per_device(
    normed, gate_w, up_w, down_w, gate_pre, up_pre, block_out, value_w, q_target, grad_out
):
    contract_last = (((1,), (1,)), ((), ()))
    contract_first = (((0,), (0,)), ((), ()))
    partial_value = jnp.sum(block_out.astype(jnp.float32) * value_w[None, :], axis=1)
    value_est = lax.psum(partial_value, "row")
    out_grad = output_grad(value_w, q_target, grad_out, value_est)
    normed_all, grad_all = (
        lax.all_gather(normed, "col", axis=0, tiled=True),
        lax.all_gather(out_grad, "col", axis=0, tiled=True),
    )
    grad_rows = grad_all
    hidden_grad = lax.psum_scatter(
        lax.dot_general(grad_rows, down_w, contract_last, preferred_element_type=jnp.float32),
        "row",
        scatter_dimension=0,
        tiled=True,
    )
    gate_back, up_back, act_out = swiglu_back(hidden_grad, gate_pre, up_pre)
    accumulate_gate_back = lax.all_gather(gate_back, "row", axis=0, tiled=True)
    accumulate_up_back = lax.all_gather(up_back, "row", axis=0, tiled=True)
    accumulate_act_out = lax.all_gather(act_out, "row", axis=0, tiled=True)
    grad_rows = grad_all
    gate_acc = lax.dot_general(
        normed_all, accumulate_gate_back, contract_first, preferred_element_type=jnp.float32
    )
    up_acc = lax.dot_general(
        normed_all, accumulate_up_back, contract_first, preferred_element_type=jnp.float32
    )
    down_acc = lax.dot_general(
        accumulate_act_out, grad_rows, contract_first, preferred_element_type=jnp.float32
    )
    input_term = lax.dot_general(
        accumulate_gate_back, gate_w, contract_last, preferred_element_type=jnp.float32
    )
    input_term = input_term + lax.dot_general(
        accumulate_up_back, up_w, contract_last, preferred_element_type=jnp.float32
    )
    totals = (gate_acc, up_acc, down_acc, input_term)
    grad_gate, grad_up, grad_down, input_part = totals
    grad_normed = lax.psum_scatter(input_part, "col", scatter_dimension=0, tiled=True).astype(
        jnp.bfloat16
    )
    return (
        grad_normed,
        grad_gate.astype(jnp.bfloat16),
        grad_up.astype(jnp.bfloat16),
        grad_down.astype(jnp.bfloat16),
    )


def solution(mesh):
    return jax.shard_map(
        per_device,
        mesh=mesh,
        in_specs=(
            P("col", "row"),
            P("row", "col"),
            P("row", "col"),
            P("col", "row"),
            P("row", "col"),
            P("row", "col"),
            P("col", "row"),
            P("row"),
            P("col"),
            P("col", "row"),
        ),
        out_specs=(P("col", "row"), P("row", "col"), P("row", "col"), P("col", "row")),
        check_vma=False,
    )
```

profile of v0, /device:TPU:64, one launch (start us, length us, event | category | flops | bytes accessed | tf_op | source)
XLA Modules:
  0.0 540.2 jit_solution(3005882080864277036)
XLA Ops:
  7.2 0.0 copy-start
  7.2 0.0 reduce-scatter.8.cloned.1.call-start
  7.2 0.9 multiply_reduce_fusion
  8.1 57.8 %psum.7 = f32[48]{0:T(128)S(1)} all-reduce(f32[48]{0:T(128)S(1)} %multiply_reduce_fusion), channel_id=1, replica_groups=mesh['row'=32,'col'=16] {'row'}, use_global_device_ids=true, to_apply=%region_1.0 | all-reduce | flops 48 | bytes 384 | tf_op jit(solution)/shard_map/psum | solution.py:38
  65.9 0.7 fusion.11
  66.5 0.8 add_convert_fusion
  67.3 46.0 %all_gather.15 = bf16[768,256]{1,0:T(8,128)(2,1)S(1)} all-gather(bf16[48,256]{1,0:T(8,128)(2,1)S(1)} %add_convert_fusion), channel_id=1, replica_groups=mesh['row'=32,'col'=16] {'col'}, dimensions={0}, use_global_device_ids=true | all-gather | bytes 417792 | tf_op jit(solution)/shard_map/all_gather | solution.py:42
  113.4 2.1 fusion.12
  115.5 0.0 reduce-scatter.8.cloned.1.call-update
  115.5 0.0 all-gather.4.cloned.1.call-start
  115.6 114.9 %reduce-scatter.8.cloned.1.call-done = f32[24,896]{1,0:T(8,128)} async-done(((f32[768,896]{1,0:T(8,128)}), f32[24,896]{1,0:T(8,128)}) %reduce-scatter.8.cloned.1.call-update) | async-done | bytes 86032
  230.5 1.6 multiply_convert_fusion
  232.1 0.0 all-gather.4.cloned.1.call-update
  232.1 0.0 all-gather.6.cloned.1.call-start
  232.1 0.7 all-gather.6.cloned.1.call-update
  232.8 0.0 all-gather.8.cloned.1.call-start
  232.9 0.5 all-gather.8.cloned.1.call-update
  233.4 0.0 reduce-scatter.6.cloned.1.call-start
  233.4 65.1 %all-gather.4.cloned.1.call-done = bf16[768,896]{1,0:T(8,128)(2,1)} async-done(((bf16[24,896]{1,0:T(8,128)(2,1)}), bf16[768,896]{1,0:T(8,128)(2,1)}) %all-gather.4.cloned.1.call-update) | async-done | bytes 1376272 | tf_op jit(solution)/shard_map/all_gather | solution.py:52
  298.5 1.9 fusion.13
  300.5 67.4 %all-gather.6.cloned.1.call-done = bf16[768,896]{1,0:T(8,128)(2,1)} async-done(((bf16[24,896]{1,0:T(8,128)(2,1)}), bf16[768,896]{1,0:T(8,128)(2,1)}) %all-gather.6.cloned.1.call-update) | async-done | bytes 1376272 | tf_op jit(solution)/shard_map/all_gather | solution.py:53
  367.9 2.8 convolution_add_fusion
  370.7 0.0 reduce-scatter.6.cloned.1.call-update
  370.7 46.6 %all_gather.18 = bf16[768,256]{1,0:T(8,128)(2,1)S(1)} all-gather(bf16[48,256]{1,0:T(8,128)(2,1)S(1)} %copy-done.6), channel_id=1, replica_groups=mesh['row'=32,'col'=16] {'col'}, dimensions={0}, use_global_device_ids=true | all-gather | bytes 417792 | tf_op jit(solution)/shard_map/all_gather | solution.py:41
  417.3 0.6 fusion
  417.9 1.0 copy.16
  418.9 1.9 fusion.1
  420.8 1.0 copy.17
  421.8 14.8 %all-gather.8.cloned.1.call-done = bf16[768,896]{1,0:T(8,128)(2,1)} async-done(((bf16[24,896]{1,0:T(8,128)(2,1)}), bf16[768,896]{1,0:T(8,128)(2,1)}) %all-gather.8.cloned.1.call-update) | async-done | bytes 1376272 | tf_op jit(solution)/shard_map/all_gather | solution.py:54
  436.6 2.7 convolution_convert_fusion
  439.2 93.1 %reduce-scatter.6.cloned.1.call-done = f32[48,256]{1,0:T(8,128)} async-done(((f32[768,256]{1,0:T(8,128)}), f32[48,256]{1,0:T(8,128)}) %reduce-scatter.6.cloned.1.call-update) | async-done | bytes 49168 | tf_op jit(solution)/shard_map/reduce_scatter | solution.py:73
  532.3 1.4 convert_element_type.49
  (13 shorter events, 0.0 us)
Async XLA Ops:
  7.2 106.2 %copy-start = (bf16[896,256]{1,0:T(8,128)(2,1)S(1)}, bf16[896,256]{1,0:T(8,128)(2,1)}, u32[]{:S(2)}) copy-start(bf16[896,256]{1,0:T(8,128)(2,1)} %param.13) | copy-start | bytes 1376260
  7.2 223.3 %reduce-scatter.8.cloned.1.call-start = ((), (), s32[]{:S(2)}) async-start(), calls=%async_computation.6 | async-start | bytes 2838528
  115.5 115.0 %copy-start.4 = (bf16[24,896]{1,0:T(8,128)(2,1)S(1)}, bf16[24,896]{1,0:T(8,128)(2,1)}, u32[]{:S(2)}) copy-start(bf16[24,896]{1,0:T(8,128)(2,1)} %param.14) | copy-start | bytes 129028
  115.5 115.0 %copy-start.5 = (bf16[24,896]{1,0:T(8,128)(2,1)S(1)}, bf16[24,896]{1,0:T(8,128)(2,1)}, u32[]{:S(2)}) copy-start(bf16[24,896]{1,0:T(8,128)(2,1)} %param.15) | copy-start | bytes 129028
  115.5 183.0 %copy-start.2 = (bf16[256,896]{1,0:T(8,128)(2,1)S(1)}, bf16[256,896]{1,0:T(8,128)(2,1)}, u32[]{:S(2)}) copy-start(bf16[256,896]{1,0:T(8,128)(2,1)} %param.11) | copy-start | bytes 1376260
  115.5 183.0 %all-gather.4.cloned.1.call-start = ((), (), s32[]{:S(2)}) async-start(), calls=%async_computation.2 | async-start | bytes 1419264 | tf_op jit(solution)/shard_map/all_gather | solution.py:52
  232.0 135.8 %copy-start.3 = (bf16[256,896]{1,0:T(8,128)(2,1)S(1)}, bf16[256,896]{1,0:T(8,128)(2,1)}, u32[]{:S(2)}) copy-start(bf16[256,896]{1,0:T(8,128)(2,1)} %param.12) | copy-start | bytes 1376260
  232.1 135.8 %all-gather.6.cloned.1.call-start = ((), (), s32[]{:S(2)}) async-start(), calls=%async_computation.3 | async-start | bytes 1419264 | tf_op jit(solution)/shard_map/all_gather | solution.py:53
  232.8 203.7 %all-gather.8.cloned.1.call-start = ((), (), s32[]{:S(2)}) async-start(), calls=%async_computation.5 | async-start | bytes 1419264 | tf_op jit(solution)/shard_map/all_gather | solution.py:54
  233.4 298.9 %reduce-scatter.6.cloned.1.call-start = ((), (), s32[]{:S(2)}) async-start(), calls=%async_computation.4 | async-start | bytes 835584 | tf_op jit(solution)/shard_map/reduce_scatter | solution.py:73
  300.5 70.3 %copy-start.6 = (bf16[48,256]{1,0:T(8,128)(2,1)S(1)}, bf16[48,256]{1,0:T(8,128)(2,1)}, u32[]{:S(2)}) copy-start(bf16[48,256]{1,0:T(8,128)(2,1)} %param.10) | copy-start | bytes 73732
  300.5 116.9 %copy-start.1 = (bf16[768,896]{1,0:T(8,128)(2,1)S(1)}, bf16[768,896]{1,0:T(8,128)(2,1)}, u32[]{:S(2)}) copy-start(bf16[768,896]{1,0:T(8,128)(2,1)} %all-gather.4.cloned.1.call-done) | copy-start | bytes 4128772
Sparse Core Ops, SparseCore 0:
  115.7 114.7 reduce-scatter.7
  233.2 65.2 all-gather.3
  301.2 66.5 all-gather.5
  369.9 66.6 all-gather.7
  440.5 91.7 reduce-scatter.5
where the time goes:
time: 541 us; the launch traced here: 540 us
  waiting for transfers between devices  356 us (66%)
  blocking collectives  150 us (28%)
  between operations  13.8 us (3%)
  matrix products  12.1 us (2%)
    unnamed x6, waiting for transfers between devices  116 us
    reduce_scatter x1, waiting for transfers between devices, per_device(): lax.psum_scatter(input_part, 'col', scatter_dimension=0, tiled=True)  93.1 us
    all_gather x1, waiting for transfers between devices, per_device(): accumulate_up_back = lax.all_gather(up_back, 'row', axis=0, tiled=True)  67.4 us
    all_gather x1, waiting for transfers between devices, per_device(): accumulate_gate_back = lax.all_gather(gate_back, 'row', axis=0, tiled=True)  65.1 us
    psum x1, blocking collectives, per_device(): value_est = lax.psum(partial_value, 'row')  57.8 us
    all_gather x1, blocking collectives, per_device(): lax.all_gather(normed, 'col', axis=0, tiled=True)  46.6 us
    all_gather x1, blocking collectives, per_device(): lax.all_gather(out_grad, 'col', axis=0, tiled=True)  46 us
    all_gather x1, waiting for transfers between devices, per_device(): accumulate_act_out = lax.all_gather(act_out, 'row', axis=0, tiled=True)  14.8 us
  transfers between devices with their start and end apart: 5, of which 5 were waited for; matrix products, arithmetic and copies ran while one was open for 2% of the time, Pallas kernels for 0%

commit v1 on v0

v1 whole, which is shorter than its diff:
```python
import jax
import jax.numpy as jnp
from jax import lax
from jax.experimental import pallas as pl
from jax.experimental.pallas import tpu as pltpu
from jax.sharding import PartitionSpec as P

expectile = 0.7
value_scale = 8.0

F32 = jnp.float32
BF16 = jnp.bfloat16
CUT = 512
N_COPIES = 256

NT = (((1,), (1,)), ((), ()))
TN = (((0,), (0,)), ((), ()))


def dot_nt(a, b):
    return lax.dot_general(a, b, NT, preferred_element_type=F32)


def dot_tn(a, b):
    return lax.dot_general(a, b, TN, preferred_element_type=F32)


def kernel(
    normed_h, gate_w_h, up_w_h, down_w_h, gate_pre, up_pre, block_out, value_w, q_target, grad_out_h,
    o_normed, o_gate, o_up, o_down,
    GO, NO, GU, gw, uw, dw,
    PK, SIN, PO, SB, RA1, RA2, RB1, RB2, RF, YS, YR, HA,
    SIL, GF, ACT, GB, UB, OG,
    CS, RX, TS, RY,
    M0, MS, M1, MY, M2, MZ, VG, U,
    local, ss, rs,
):
    row, col = lax.axis_index("row"), lax.axis_index("col")
    k, z, yl = row % 2, (row // 2) % 8, row // 16
    x, yh = col % 4, col // 4

    def dev(k_=k, z_=z, yl_=yl, x_=x, yh_=yh):
        return ((yl_ * 8 + z_) * 2 + k_, yh_ * 4 + x_)

    def zd(d):
        return (z + d + 8) % 8

    def xd(d):
        return (x + d + 4) % 4

    def yd(d):
        return (yh + d + 4) % 4

    sib = dev(k_=1 - k)
    ylp = dev(yl_=1 - yl)
    zdev = {d: dev(z_=zd(d)) for d in (1, -1, 2, -2, 3, -3, 4)}
    xdev = {d: dev(x_=xd(d)) for d in (1, 2, 3)}
    ydev = {d: dev(yh_=yd(d)) for d in (1, 2, 3)}

    started = []

    def send(src, dst, to):
        i = len(started)
        cp = pltpu.make_async_remote_copy(
            src, dst, ss.at[i], rs.at[i], device_id=to, device_id_type=pl.DeviceIdType.MESH
        )
        cp.start()
        started.append(cp)
        return cp

    loads = []

    def load(src, dst):
        cp = pltpu.make_async_copy(src, dst, local.at[len(loads)])
        cp.start()
        loads.append(cp)
        return cp

    l_go = load(grad_out_h, GO.at[col])
    l_dw = load(down_w_h, dw)
    l_no = load(normed_h, NO.at[col])
    l_gw = load(gate_w_h, gw)
    l_uw = load(up_w_h, uw)

    barrier = pltpu.get_barrier_semaphore()
    partners = [sib, ylp, *zdev.values(), *xdev.values(), *ydev.values()]
    for p in partners:
        pl.semaphore_signal(barrier, inc=1, device_id=p, device_id_type=pl.DeviceIdType.MESH)

    GU[row] = jnp.concatenate([gate_pre[...].astype(F32), up_pre[...].astype(F32)], axis=0).astype(BF16)
    l_go.wait()
    pl.semaphore_wait(barrier, len(partners))

    def gather_y(buf):
        cy = {d: send(buf.at[col], buf.at[col], ydev[d]) for d in (1, 3, 2)}
        cx = {(0, d): send(buf.at[col], buf.at[col], xdev[d]) for d in (1, 3, 2)}
        return cy, cx

    def gather_x(buf, cy, cx):
        for dy in (1, 3, 2):
            cy[dy].wait_recv()
            at = yd(-dy) * 4 + x
            for d in (1, 3, 2):
                cx[(dy, d)] = send(buf.at[at], buf.at[at], xdev[d])

    def gather_end(cx):
        for cp in cx.values():
            cp.wait_recv()

    def z_start(buf, at):
        a = at(0)
        return {d: send(buf.at[a], buf.at[a], zdev[d]) for d in (2, -2, 1, -1)}

    def z_relay(buf, at, st):
        out = {}
        st[2].wait_recv()
        a = at(-2)
        out[3] = send(buf.at[a], buf.at[a], zdev[1])
        out["a"] = send(buf.at[a, :, :CUT], buf.at[a, :, :CUT], zdev[2])
        st[-2].wait_recv()
        a = at(2)
        out[-3] = send(buf.at[a], buf.at[a], zdev[-1])
        out["b"] = send(buf.at[a, :, CUT:], buf.at[a, :, CUT:], zdev[-2])
        return out

    cy, cx = gather_y(GO)

    def gu_at(kk, yy):
        return lambda d: (yy * 8 + zd(d)) * 2 + kk

    mine = gu_at(k, yl)
    st = z_start(GU, mine)
    gu_y, gu_s, gu_s2 = {}, {}, {}

    def gu_forward(d):
        a = mine(d)
        gu_y[d] = send(GU.at[a], GU.at[a], ylp)
        gu_s[d] = send(GU.at[a], GU.at[a], sib)

    def gu_forward2(d):
        gu_y[d].wait_recv()
        a = gu_at(k, 1 - yl)(d)
        gu_s2[d] = send(GU.at[a], GU.at[a], sib)

    gu_forward(0)

    l_dw.wait()
    vw = value_w[...]
    hi = vw.astype(BF16).astype(F32)
    mid = (vw - hi).astype(BF16).astype(F32)
    lo = vw - hi - mid
    terms = jnp.concatenate([hi, mid, lo, jnp.zeros((5, 256), F32)], axis=0).astype(BF16)
    u_part = jnp.sum(dot_nt(terms, dw[...]), axis=0, keepdims=True)
    v_part = jnp.sum(dot_nt(terms, block_out[...]), axis=0, keepdims=True)
    M0[...] = jnp.zeros((8, 128), F32)
    for i in range(7):
        M0[i : i + 1, :] = u_part[:, 128 * i : 128 * (i + 1)]
    M0[7:8, 0:48] = v_part
    m_s = send(M0, MS, sib)

    gather_x(GO, cy, cx)

    m_s.wait_recv()
    M1[...] = M0[...] + MS[...]
    m_y = send(M1, MY, ylp)

    relay = z_relay(GU, mine, st)

    m_y.wait_recv()
    M2[...] = M1[...] + MY[...]
    m_z = [send(M2, MZ.at[i], zdev[d]) for i, d in enumerate((4, 3, -3, 2, -2, 1, -1))]

    gu_forward(-2)
    gu_forward(2)
    st[1].wait_recv()
    gu_forward(-1)
    st[-1].wait_recv()
    gu_forward(1)

    gather_end(cx)

    order = (3, -3, 4, 2, -2, 1, -1, 0)
    slot = {d: i for i, d in enumerate(order)}
    sib_copy = {}
    for d0, d1 in ((3, -3), (4, 2), (-2, 1), (-1, 0)):
        a = jnp.concatenate([GO[(1 - k) * 8 + zd(d0)], GO[(1 - k) * 8 + zd(d1)]], axis=0)
        p = dot_nt(a, dw[...]).astype(BF16)
        PK[slot[d0]] = p[:48]
        PK[slot[d1]] = p[48:]
        sib_copy[d0] = send(PK.at[slot[d0]], SIN.at[slot[d0]], sib)
        sib_copy[d1] = send(PK.at[slot[d1]], SIN.at[slot[d1]], sib)
    for d0, d1 in ((3, -3), (4, 2), (-2, 1), (-1, 0)):
        a = jnp.concatenate([GO[k * 8 + zd(d0)], GO[k * 8 + zd(d1)]], axis=0)
        p = dot_nt(a, dw[...])
        PO[slot[d0]] = p[:48]
        PO[slot[d1]] = p[48:]

    def pair_sum(d):
        sib_copy[d].wait_recv()
        return PO[slot[d]] + SIN[slot[d]].astype(F32)

    SB[slot[3]] = pair_sum(3).astype(BF16)
    r_a1 = send(SB.at[slot[3]], RA1, zdev[1])
    SB[slot[-3]] = pair_sum(-3).astype(BF16)
    r_b1 = send(SB.at[slot[-3]], RB1, zdev[-1])
    SB[slot[4]] = pair_sum(4).astype(BF16)
    r_a2 = send(SB.at[slot[4], :, :CUT], RA2, zdev[2])
    r_b2 = send(SB.at[slot[4], :, CUT:], RB2, zdev[-2])
    SB[slot[1]] = pair_sum(1).astype(BF16)
    f_1 = send(SB.at[slot[1]], RF.at[0], zdev[1])
    SB[slot[-1]] = pair_sum(-1).astype(BF16)
    f_m1 = send(SB.at[slot[-1]], RF.at[1], zdev[-1])
    s2 = pair_sum(2)
    r_a1.wait_recv()
    r_a2.wait_recv()
    SB[slot[2], :, :CUT] = (s2[:, :CUT] + RA1[:, :CUT].astype(F32) + RA2[...].astype(F32)).astype(BF16)
    SB[slot[2], :, CUT:] = (s2[:, CUT:] + RA1[:, CUT:].astype(F32)).astype(BF16)
    f_2 = send(SB.at[slot[2]], RF.at[2], zdev[2])
    sm2 = pair_sum(-2)
    r_b1.wait_recv()
    r_b2.wait_recv()
    SB[slot[-2], :, :CUT] = (sm2[:, :CUT] + RB1[:, :CUT].astype(F32)).astype(BF16)
    SB[slot[-2], :, CUT:] = (sm2[:, CUT:] + RB1[:, CUT:].astype(F32) + RB2[...].astype(F32)).astype(BF16)
    f_m2 = send(SB.at[slot[-2]], RF.at[3], zdev[-2])

    l_no.wait()
    ny, nx = gather_y(NO)
    relay[3].wait_recv()
    gu_forward(-3)
    relay[-3].wait_recv()
    gu_forward(3)
    relay["a"].wait_recv()
    relay["b"].wait_recv()
    gu_forward(4)
    for cp in m_z:
        cp.wait_recv()
    total = M2[...]
    for i in range(7):
        total = total + MZ[i]
    for i in range(7):
        U[:, 128 * i : 128 * (i + 1)] = total[i : i + 1, :]
    margin = q_target[...] - total[7:8, 0:48]
    weighting = jnp.where(margin > 0, expectile, 1.0 - expectile)
    VG[col] = jnp.zeros((8, 128), F32)
    VG[col, 0:1, 0:48] = -2.0 * value_scale * weighting * margin
    vy, vx = gather_y(VG)
    gather_x(NO, ny, nx)
    for d in (0, -2, 2, -1, 1, -3, 3, 4):
        gu_forward2(d)
    gather_x(VG, vy, vx)

    for cp in (f_1, f_m1, f_2, f_m2):
        cp.wait_recv()
    s0 = pair_sum(0)
    for i in range(4):
        s0 = s0 + RF[i].astype(F32)
    YS[...] = s0.astype(BF16)
    y_c = send(YS, YR, ylp)

    for d in (0, -2, 2, -1, 1, -3, 3, 4):
        gu_s[d].wait_recv()
        gu_s2[d].wait_recv()

    def factors(j, carry):
        a = GU[2 * j].astype(F32)
        b = GU[2 * j + 1].astype(F32)
        gate = jnp.concatenate([a[:24], b[:24]], axis=0)
        up = jnp.concatenate([a[24:], b[24:]], axis=0)
        s = jax.nn.sigmoid(gate)
        silu = gate * s
        SIL[j] = silu
        ACT[j] = (silu * up).astype(BF16)
        GF[j] = up * s * (1.0 + gate * (1.0 - s))
        return carry

    lax.fori_loop(0, 8, factors, 0)

    y_c.wait_recv()
    me = k * 8 + z
    HA[me] = (YS[...].astype(F32) + YR[...].astype(F32)).astype(BF16)

    def h_at(d):
        return k * 8 + zd(d)

    hst = z_start(HA, h_at)
    h_s = {}

    def h_forward(d):
        h_s[d] = send(HA.at[h_at(d)], HA.at[h_at(d)], sib)

    h_forward(0)
    lax.fori_loop(8, 12, factors, 0)
    hrel = z_relay(HA, h_at, hst)
    h_forward(-2)
    h_forward(2)
    hst[1].wait_recv()
    h_forward(-1)
    hst[-1].wait_recv()
    h_forward(1)
    lax.fori_loop(12, 16, factors, 0)

    gather_end(vx)

    def value_col(j):
        return VG[j].T[:48, 0:1]

    def out_grad(j, carry):
        OG[j] = (GO[j].astype(F32) + value_col(j) * vw).astype(BF16)
        return carry

    lax.fori_loop(0, 16, out_grad, 0)
    o_down[...] = dot_tn(ACT[...].reshape(768, 896), OG[...].reshape(768, 256)).astype(BF16)

    hrel[3].wait_recv()
    h_forward(-3)
    hrel[-3].wait_recv()
    h_forward(3)
    hrel["a"].wait_recv()
    hrel["b"].wait_recv()
    h_forward(4)
    for cp in h_s.values():
        cp.wait_recv()

    l_gw.wait()
    l_uw.wait()

    def back(j):
        h = HA[j].astype(F32) + value_col(j) * U[...]
        GB[j] = (h * GF[j]).astype(BF16)
        UB[j] = (h * SIL[j]).astype(BF16)

    own = None
    x_c = {}
    for d in (2, 1, 3, 0):
        for q in range(4):
            back(q * 4 + xd(d))
        g = jnp.concatenate([GB[q * 4 + xd(d)] for q in range(4)], axis=0)
        u = jnp.concatenate([UB[q * 4 + xd(d)] for q in range(4)], axis=0)
        part = (dot_nt(g, gw[...]) + dot_nt(u, uw[...])).reshape(4, 48, 256)
        if d:
            CS[d - 1] = part.astype(BF16)
            x_c[d] = send(CS.at[d - 1], RX.at[d - 1], xdev[d])
        else:
            own = part
    gather_end(nx)
    o_gate[...] = dot_tn(NO[...].reshape(768, 256), GB[...].reshape(768, 896)).astype(BF16)
    for d in (1, 2, 3):
        x_c[d].wait_recv()
        own = own + RX[d - 1].astype(F32)
    TS[...] = own
    y_s = {}
    for d in (2, 1, 3):
        CS[3, d] = TS[yd(d)].astype(BF16)
        y_s[d] = send(CS.at[3, d], RY.at[d - 1], ydev[d])
    o_up[...] = dot_tn(NO[...].reshape(768, 256), UB[...].reshape(768, 896)).astype(BF16)
    out = TS[yh]
    for d in (1, 2, 3):
        y_s[d].wait_recv()
        out = out + RY[d - 1].astype(F32)
    o_normed[...] = out.astype(BF16)

    for cp in started:
        cp.wait_send()


def per_device(normed, gate_w, up_w, down_w, gate_pre, up_pre, block_out, value_w, q_target, grad_out):
    hbm = pl.BlockSpec(memory_space=pl.ANY)
    vmem = pl.BlockSpec(memory_space=pltpu.VMEM)
    scratch = [
        pltpu.VMEM((16, 48, 256), BF16),
        pltpu.VMEM((16, 48, 256), BF16),
        pltpu.VMEM((32, 48, 896), BF16),
        pltpu.VMEM((256, 896), BF16),
        pltpu.VMEM((256, 896), BF16),
        pltpu.VMEM((896, 256), BF16),
        pltpu.VMEM((8, 48, 896), BF16),
        pltpu.VMEM((8, 48, 896), BF16),
        pltpu.VMEM((8, 48, 896), F32),
        pltpu.VMEM((8, 48, 896), BF16),
        pltpu.VMEM((48, 896), BF16),
        pltpu.VMEM((48, CUT), BF16),
        pltpu.VMEM((48, 896), BF16),
        pltpu.VMEM((48, 896 - CUT), BF16),
        pltpu.VMEM((4, 48, 896), BF16),
        pltpu.VMEM((48, 896), BF16),
        pltpu.VMEM((48, 896), BF16),
        pltpu.VMEM((16, 48, 896), BF16),
        pltpu.VMEM((16, 48, 896), F32),
        pltpu.VMEM((16, 48, 896), F32),
        pltpu.VMEM((16, 48, 896), BF16),
        pltpu.VMEM((16, 48, 896), BF16),
        pltpu.VMEM((16, 48, 896), BF16),
        pltpu.VMEM((16, 48, 256), BF16),
        pltpu.VMEM((4, 4, 48, 256), BF16),
        pltpu.VMEM((3, 4, 48, 256), BF16),
        pltpu.VMEM((4, 48, 256), F32),
        pltpu.VMEM((3, 48, 256), BF16),
        pltpu.VMEM((8, 128), F32),
        pltpu.VMEM((8, 128), F32),
        pltpu.VMEM((8, 128), F32),
        pltpu.VMEM((8, 128), F32),
        pltpu.VMEM((8, 128), F32),
        pltpu.VMEM((7, 8, 128), F32),
        pltpu.VMEM((16, 8, 128), F32),
        pltpu.VMEM((1, 896), F32),
        pltpu.SemaphoreType.DMA((5,)),
        pltpu.SemaphoreType.DMA((N_COPIES,)),
        pltpu.SemaphoreType.DMA((N_COPIES,)),
    ]
    return pl.pallas_call(
        kernel,
        out_shape=(
            jax.ShapeDtypeStruct((48, 256), BF16),
            jax.ShapeDtypeStruct((256, 896), BF16),
            jax.ShapeDtypeStruct((256, 896), BF16),
            jax.ShapeDtypeStruct((896, 256), BF16),
        ),
        in_specs=[hbm, hbm, hbm, hbm, vmem, vmem, vmem, vmem, vmem, hbm],
        out_specs=(vmem, vmem, vmem, vmem),
        scratch_shapes=scratch,
        compiler_params=pltpu.CompilerParams(
            collective_id=0, has_side_effects=True, vmem_limit_bytes=48 * 2**20
        ),
    )(
        normed, gate_w, up_w, down_w, gate_pre, up_pre, block_out,
        value_w.reshape(1, 256), q_target.reshape(1, 48), grad_out,
    )


def solution(mesh):
    return jax.shard_map(
        per_device,
        mesh=mesh,
        in_specs=(
            P("col", "row"),
            P("row", "col"),
            P("row", "col"),
            P("col", "row"),
            P("row", "col"),
            P("row", "col"),
            P("col", "row"),
            P("row"),
            P("col"),
            P("col", "row"),
        ),
        out_specs=(P("col", "row"), P("row", "col"), P("row", "col"), P("col", "row")),
        check_vma=False,
    )
```

time: 541 us -> 87.2 us (0.16)
  the two profiles are of different devices: /device:TPU:64 before, /device:TPU:70 now
where the time goes in v1:
time: 87.2 us; the launch traced here: 86.7 us
  Pallas kernels  75.6 us (87%)
  local copies, waits for them, and re-layouts  10.4 us (12%)
    pallas_call x1, Pallas kernels, per_device(): pl.pallas_call(kernel, out_shape=(jax.ShapeDtypeStruct((48, 256), BF16),...  75.6 us
    unnamed x24, local copies, waits for them, and re-layouts  10.4 us

profile of v1, /device:TPU:70, one launch (start us, length us, event | category | flops | bytes accessed | tf_op | source)
XLA Modules:
  0.0 86.7 jit_solution(11286431344210639515)
XLA Ops:
  0.6 0.0 copy-start.8
  0.6 0.0 copy-start.9
  0.7 0.7 copy-done.8
  1.3 0.0 copy-done.9
  1.3 0.0 copy-start
  1.3 1.0 %copy-done = bf16[256,896]{1,0:T(8,128)(2,1)S(1)} copy-done((bf16[256,896]{1,0:T(8,128)(2,1)S(1)}, bf16[256,896]{1,0:T(8,128)(2,1)}, u32[]{:S(2)}) %copy-start) | copy-done | bytes 458776
  2.3 0.0 copy-start.1
  2.3 1.0 %copy-done.1 = bf16[256,896]{1,0:T(8,128)(2,1)S(1)} copy-done((bf16[256,896]{1,0:T(8,128)(2,1)S(1)}, bf16[256,896]{1,0:T(8,128)(2,1)}, u32[]{:S(2)}) %copy-start.1) | copy-done | bytes 458776
  3.4 0.0 copy-start.2
  3.4 1.0 %copy-done.2 = bf16[896,256]{1,0:T(8,128)(2,1)S(1)} copy-done((bf16[896,256]{1,0:T(8,128)(2,1)S(1)}, bf16[896,256]{1,0:T(8,128)(2,1)}, u32[]{:S(2)}) %copy-start.2) | copy-done | bytes 458776
  4.4 0.0 copy-start.3
  4.4 0.8 copy-done.3
  5.2 0.0 copy-start.4
  5.2 0.8 copy-done.4
  5.9 0.0 copy-start.5
  5.9 0.7 copy-done.5
  6.7 0.0 copy-start.6
  6.7 0.7 copy-done.6
  7.4 0.0 copy-start.7
  7.4 0.7 copy-done.7
  8.2 75.6 %shard_map.129 = (bf16[48,256]{1,0:T(8,128)(2,1)S(1)}, bf16[256,896]{1,0:T(8,128)(2,1)S(1)}, bf16[256,896]{1,0:T(8,128)(2,1)S(1)}, bf16[896,256]{1,0:T(8,128)(2,1)S(1)}) custom-call(bf16[48,256]{1,0:T(8,128)(2,1)S(1)} %copy-done.5, bf16[256,896]{1,0:T(8,128)(2,1)S(1)} %copy-done, bf16[256,896]{1,0:T(8,128)(2,1)S(1)} %copy-done.1, ...), custom_call_target="tpu_custom_call" | custom-call | tf_op jit(solution)/shard_map/pallas_call | solution.py:410
  83.8 0.6 copy.18
  84.4 0.8 copy.19
  85.1 0.8 copy.20
  85.9 0.8 copy.21
Async XLA Ops:
  0.6 0.7 copy-start.8
  0.6 0.7 copy-start.9
  1.3 1.0 %copy-start = (bf16[256,896]{1,0:T(8,128)(2,1)S(1)}, bf16[256,896]{1,0:T(8,128)(2,1)}, u32[]{:S(2)}) copy-start(bf16[256,896]{1,0:T(8,128)(2,1)} %gate_w_h.1) | copy-start | bytes 1376260
  2.3 1.0 %copy-start.1 = (bf16[256,896]{1,0:T(8,128)(2,1)S(1)}, bf16[256,896]{1,0:T(8,128)(2,1)}, u32[]{:S(2)}) copy-start(bf16[256,896]{1,0:T(8,128)(2,1)} %up_w_h.1) | copy-start | bytes 1376260
  3.4 1.0 %copy-start.2 = (bf16[896,256]{1,0:T(8,128)(2,1)S(1)}, bf16[896,256]{1,0:T(8,128)(2,1)}, u32[]{:S(2)}) copy-start(bf16[896,256]{1,0:T(8,128)(2,1)} %down_w_h.1) | copy-start | bytes 1376260
  4.4 0.8 copy-start.3
  5.2 0.8 copy-start.4
  5.9 0.7 copy-start.5
  6.7 0.7 copy-start.6
  7.4 0.7 copy-start.7

commit v2 on v0

v2 whole, which is shorter than its diff:
```python
import jax
import jax.numpy as jnp
from jax import lax
from jax.experimental import pallas as pl
from jax.experimental.pallas import tpu as pltpu
from jax.sharding import PartitionSpec as P

expectile = 0.7
value_scale = 8.0

F32 = jnp.float32
BF16 = jnp.bfloat16
MESH = pl.DeviceIdType.MESH

PARTS = ((0, 256, 512), (512, 640, 896))
CUT = 512
N_SEND = 16
N_RECV = 56
N_LOCAL = 9
DIRECT = False

NT = (((1,), (1,)), ((), ()))
TN = (((0,), (0,)), ((), ()))

def dot_nt(a, b):
    return lax.dot_general(a, b, NT, preferred_element_type=F32)

def dot_tn(a, b):
    return lax.dot_general(a, b, TN, preferred_element_type=F32)

def dot(a, b):
    return jnp.dot(a, b, preferred_element_type=F32)

def kernel(
    normed_h, gate_w_h, up_w_h, down_w_h, gate_pre, up_pre, block_out, value_w, q_target, grad_out_h,
    o_normed_h, o_gate_h, o_up_h, o_down_h,
    GO, NO, GU, gw, uw, dw, GWT, UWT, NOT,
    PK, SIN, PO, SB, RA1, RA2, RB1, RB2, RF, OWNH, YS, YR, HA,
    SIL, GF, ACT, GB, UB, OG,
    CS, RIN, OWN, o_normed, o_gate, o_up, o_down,
    M0, MS, M1, MY, M2, MZ, VG, VC, U,
    local, ss, rs,
):
    row, col = lax.axis_index("row"), lax.axis_index("col")
    k, z, yl = row % 2, (row // 2) % 8, row // 16
    x, yh = col % 4, col // 4

    def dev(k_=k, z_=z, yl_=yl, x_=x, yh_=yh):
        return ((yl_ * 8 + z_) * 2 + k_, yh_ * 4 + x_)

    def zd(d):
        return (z + d + 8) % 8

    def xd(d):
        return (x + d + 4) % 4

    def yd(d):
        return (yh + d + 4) % 4

    sib = dev(k_=1 - k)
    ylp = dev(yl_=1 - yl)
    zdev = {d: dev(z_=zd(d)) for d in (1, -1, 2, -2, 3, -3, 4)}
    xdev = {d: dev(x_=xd(d)) for d in (1, 2, 3)}
    ydev = {d: dev(yh_=yd(d)) for d in (1, 2, 3)}

    ids = {"send": {}, "recv": {}}
    started, arrived, loads = [], set(), []

    def sem(side, name):
        known = ids[side]
        if name not in known:
            known[name] = len(known)
            assert len(known) <= (N_SEND if side == "send" else N_RECV)
        return (ss if side == "send" else rs).at[known[name]]

    def remote(src, dst, group, name, to):
        return pltpu.make_async_remote_copy(
            src, dst, sem("send", group), sem("recv", name), device_id=to, device_id_type=MESH
        )

    def send(src, dst, group, name, to):
        cp = remote(src, dst, group, name, to)
        cp.start()
        started.append((cp, name))

    def came(name, ref):
        remote(ref, ref, "none", name, sib).wait_recv()
        arrived.add(name)

    def left(group, ref):
        remote(ref, ref, group, "none", sib).wait_send()

    def load(src, dst):
        cp = pltpu.make_async_copy(src, dst, local.at[len(loads)])
        cp.start()
        loads.append(cp)
        return cp

    def finish():
        for cp in loads:
            if all(cp is not w for w in waited):
                cp.wait()
        for cp, name in started:
            cp.wait_send()
            if name not in arrived:
                cp.wait_recv()

    waited = []

    def ready(*cps):
        for cp in cps:
            cp.wait()
            waited.append(cp)

    l_go = load(grad_out_h, GO.at[col])
    l_dw = load(down_w_h, dw)
    l_no = load(normed_h, NO.at[col])
    l_gw = load(gate_w_h, gw)
    l_uw = load(up_w_h, uw)

    barrier = pltpu.get_barrier_semaphore()
    partners = [sib, ylp, *zdev.values()] + [(row, (col + i) % 16) for i in range(1, 16)]
    for p in partners:
        pl.semaphore_signal(barrier, inc=1, device_id=p, device_id_type=MESH)

    GU[yl, z, k] = jnp.concatenate([gate_pre[...].astype(F32), up_pre[...].astype(F32)], axis=0).astype(BF16)
    ready(l_go)
    pl.semaphore_wait(barrier, len(partners))

    def gather_direct(buf, group, name):
        for i in (10, 6, 14, 2, 9, 11, 5, 7, 13, 15, 1, 3, 8, 4, 12):
            send(buf.at[col], buf.at[col], group, name, (row, (col + i) % 16))

    def gather_y(buf, group, name):
        for d in (2, 1, 3):
            send(buf.at[col], buf.at[col], group, name + str(d), ydev[d])
        for d in (2, 1, 3):
            send(buf.at[col], buf.at[col], group, name, xdev[d])

    def gather_x(buf, group, name):
        for dy in (1, 3, 2):
            at = yd(-dy) * 4 + x
            came(name + str(dy), buf.at[at])
            for d in (2, 1, 3):
                send(buf.at[at], buf.at[at], group, name, xdev[d])

    if DIRECT:
        gather_direct(GO, "go", "go")
    else:
        gather_y(GO, "go", "go")

    def gu(d):
        return GU.at[yl, zd(d), k]

    def gu_y(d):
        send(gu(d), gu(d), "guy", "guy", ylp)

    for d, name in ((2, "gu+2"), (-2, "gu-2"), (1, "gu1"), (-1, "gu1")):
        send(gu(0), gu(0), "guz", name, zdev[d])
    if not DIRECT:
        gu_y(0)

    ready(l_dw)
    vw = value_w[...]
    hi = vw.astype(BF16).astype(F32)
    mid = (vw - hi).astype(BF16).astype(F32)
    lo = vw - hi - mid
    terms = jnp.concatenate([hi, mid, lo, jnp.zeros((5, 256), F32)], axis=0).astype(BF16)
    u_part = jnp.sum(dot_nt(terms, dw[...]), axis=0, keepdims=True)
    v_part = jnp.sum(dot_nt(terms, block_out[...]), axis=0, keepdims=True)
    M0[...] = jnp.zeros((8, 128), F32)
    for i in range(7):
        M0[i : i + 1, :] = u_part[:, 128 * i : 128 * (i + 1)]
    M0[7:8, 0:48] = v_part
    send(M0, MS, "m0", "m0", sib)

    if not DIRECT:
        gather_x(GO, "go", "go")

    came("m0", MS)
    M1[...] = M0[...] + MS[...]
    send(M1, MY, "m1", "m1", ylp)

    came("gu+2", gu(-2))
    send(gu(-2), gu(-2), "guz", "gu3", zdev[1])
    send(gu(-2).at[:, :CUT], gu(-2).at[:, :CUT], "guz", "gu3", zdev[2])
    came("gu-2", gu(2))
    send(gu(2), gu(2), "guz", "gu3", zdev[-1])
    send(gu(2).at[:, CUT:], gu(2).at[:, CUT:], "guz", "gu3", zdev[-2])

    came("m1", MY)
    M2[...] = M1[...] + MY[...]
    for i, d in enumerate((4, 3, -3, 2, -2, 1, -1)):
        send(M2, MZ.at[i], "m2", "m2", zdev[d])

    if not DIRECT:
        gu_y(-2)
        gu_y(2)
        came("gu1", GU.at[0, 0:2, 0])
        gu_y(-1)
        gu_y(1)

    if DIRECT:
        came("go", GO.at[0:15])
    else:
        came("go", GO.at[0:12])

    order = (3, -3, 4, 2, -2, 1, -1, 0)
    slot = {d: i for i, d in enumerate(order)}
    pairs = ((3, -3), (4, 2), (-2, 1), (-1, 0))
    for h, (lo, _, up) in enumerate(PARTS):
        for i, (d0, d1) in enumerate(pairs):
            a = jnp.concatenate([GO[(1 - k) * 8 + zd(d0)], GO[(1 - k) * 8 + zd(d1)]], axis=0)
            p = dot_nt(a, dw[lo:up]).astype(BF16)
            PK[2 * i, :, lo:up] = p[:48]
            PK[2 * i + 1, :, lo:up] = p[48:]
            at = pl.ds(2 * i, 2)
            send(PK.at[at, :, lo:up], SIN.at[at, :, lo:up], "pk", ("sin", i, h), sib)
        for i, (d0, d1) in enumerate(pairs):
            a = jnp.concatenate([GO[k * 8 + zd(d0)], GO[k * 8 + zd(d1)]], axis=0)
            p = dot_nt(a, dw[lo:up])
            PO[2 * i, :, lo:up] = p[:48]
            PO[2 * i + 1, :, lo:up] = p[48:]

    def pair_sum(d, h):
        lo, _, up = PARTS[h]
        i = slot[d] // 2
        if ("sin", i, h) not in arrived:
            came(("sin", i, h), SIN.at[pl.ds(2 * i, 2), :, lo:up])
        return PO[slot[d], :, lo:up] + SIN[slot[d], :, lo:up].astype(F32)

    def rs_first(h):
        lo, cut, up = PARTS[h]
        for d in (3, -3, 4):
            SB[slot[d], :, lo:up] = pair_sum(d, h).astype(BF16)
            src = SB.at[slot[d]]
            if d == 3:
                send(src.at[:, lo:up], RA1.at[:, lo:up], "rs", ("a1", h), zdev[1])
            elif d == -3:
                send(src.at[:, lo:up], RB1.at[:, lo:up], "rs", ("b1", h), zdev[-1])
            else:
                send(src.at[:, lo:cut], RA2.at[:, lo:cut], "rs", ("a2", h), zdev[2])
                send(src.at[:, cut:up], RB2.at[:, cut:up], "rs", ("b2", h), zdev[-2])

    def rs_near(h):
        lo, cut, up = PARTS[h]
        for i, d in enumerate((1, -1)):
            SB[slot[d], :, lo:up] = pair_sum(d, h).astype(BF16)
            send(SB.at[slot[d], :, lo:up], RF.at[i, :, lo:up], "rs", ("rf", h), zdev[d])

    def rs_second(h):
        lo, cut, up = PARTS[h]
        t = pair_sum(2, h)
        came(("a1", h), RA1.at[:, lo:up])
        came(("a2", h), RA2.at[:, lo:cut])
        t = t + RA1[:, lo:up].astype(F32)
        SB[slot[2], :, lo:cut] = (t[:, : cut - lo] + RA2[:, lo:cut].astype(F32)).astype(BF16)
        SB[slot[2], :, cut:up] = t[:, cut - lo :].astype(BF16)
        send(SB.at[slot[2], :, lo:up], RF.at[2, :, lo:up], "rs", ("rf", h), zdev[2])
        t = pair_sum(-2, h)
        came(("b1", h), RB1.at[:, lo:up])
        came(("b2", h), RB2.at[:, cut:up])
        t = t + RB1[:, lo:up].astype(F32)
        SB[slot[-2], :, lo:cut] = t[:, : cut - lo].astype(BF16)
        SB[slot[-2], :, cut:up] = (t[:, cut - lo :] + RB2[:, cut:up].astype(F32)).astype(BF16)
        send(SB.at[slot[-2], :, lo:up], RF.at[3, :, lo:up], "rs", ("rf", h), zdev[-2])

    rs_first(0)
    rs_first(1)
    rs_near(0)
    rs_second(0)
    rs_near(1)
    rs_second(1)

    if DIRECT:
        for d in (0, -2, 2):
            gu_y(d)
        came("gu1", GU.at[0, 0:2, 0])
        gu_y(-1)
        gu_y(1)
    came("gu3", GU.at[0, 0:3, 0])
    for d in (-3, 3, 4):
        gu_y(d)
    send(GU.at[yl, :, k], GU.at[yl, :, k], "gus", "gus1", sib)
    came("m2", MZ)
    total = M2[...]
    for i in range(7):
        total = total + MZ[i]
    for i in range(7):
        U[:, 128 * i : 128 * (i + 1)] = total[i : i + 1, :]
    margin = q_target[...] - total[7:8, 0:48]
    weighting = jnp.where(margin > 0, expectile, 1.0 - expectile)
    VG[col] = jnp.zeros((8, 128), F32)
    VG[col, 0:1, 0:48] = -2.0 * value_scale * weighting * margin
    gather_direct(VG, "vg", "vg")
    ready(l_no, l_gw, l_uw)
    gather_y(NO, "no", "no")
    GWT[...] = gw[...].T
    UWT[...] = uw[...].T

    for h, (lo, _, up) in enumerate(PARTS):
        t = pair_sum(0, h)
        came(("rf", h), RF.at[:, :, lo:up])
        for i in range(4):
            t = t + RF[i, :, lo:up].astype(F32)
        OWNH[:, lo:up] = t
        YS[:, lo:up] = t.astype(BF16)
        send(YS.at[:, lo:up], YR.at[:, lo:up], "y", ("y", h), ylp)

    gather_x(NO, "no", "no")

    def h_at(d):
        return k * 8 + zd(d)

    def h_send(name, a, lo, up, to):
        send(HA.at[a, :, lo:up], HA.at[a, :, lo:up], "ha", name, to)

    for h, (lo, _, up) in enumerate(PARTS):
        came(("y", h), YR.at[:, lo:up])
        HA[h_at(0), :, lo:up] = (OWNH[:, lo:up] + YR[:, lo:up].astype(F32)).astype(BF16)
        for d in (2, -2):
            h_send(("h", d, h), h_at(0), lo, up, zdev[d])
    for lo, _, up in PARTS:
        for d in (1, -1):
            h_send("h1", h_at(0), lo, up, zdev[d])

    def h_forward(name, *ds):
        for d in ds:
            send(HA.at[h_at(d)], HA.at[h_at(d)], "has", name, sib)

    h_forward("s0", 0)

    came("vg", VG.at[0:15])

    def out_grad(j, carry):
        VC[j] = jnp.broadcast_to(VG[j].T[:48, 0:1], (48, 128))
        wide = jnp.concatenate([VC[j]] * 2, axis=1)
        OG[j] = (GO[j].astype(F32) + wide * vw).astype(BF16)
        return carry

    lax.fori_loop(0, 16, out_grad, 0)
    came("guy", GU.at[1 - yl, :, k])
    send(GU.at[1 - yl, :, k], GU.at[1 - yl, :, k], "gus", "gus2", sib)

    for h, (lo, cut, up) in enumerate(PARTS):
        came(("h", 2, h), HA.at[h_at(-2), :, lo:up])
        h_send("h3", h_at(-2), lo, up, zdev[1])
        h_send("h4", h_at(-2), lo, cut, zdev[2])
        came(("h", -2, h), HA.at[h_at(2), :, lo:up])
        h_send("h3", h_at(2), lo, up, zdev[-1])
        h_send("h4", h_at(2), cut, up, zdev[-2])
    h_forward("s2", -2, 2)
    came("h1", HA.at[0:2])
    h_forward("s1", -1, 1)

    came("gus1", GU.at[yl, :, 1 - k])
    came("gus2", GU.at[1 - yl, :, 1 - k])

    def factors(j, carry):
        a = GU[j // 8, j % 8, 0].astype(F32)
        b = GU[j // 8, j % 8, 1].astype(F32)
        gate = jnp.concatenate([a[:24], b[:24]], axis=0)
        up = jnp.concatenate([a[24:], b[24:]], axis=0)
        s = jax.nn.sigmoid(gate)
        silu = gate * s
        SIL[j] = silu
        ACT[j] = (silu * up).astype(BF16)
        GF[j] = up * s * (1.0 + gate * (1.0 - s))
        return carry

    lax.fori_loop(0, 16, factors, 0)

    def tokens(name, *ds):
        if name is not None:
            came(name, HA.at[pl.ds(0, len(ds))])
        js = [j for d in ds for j in (k * 8 + zd(d), (1 - k) * 8 + zd(d))]
        for j in js:
            h = HA[j].astype(F32) + jnp.concatenate([VC[j]] * 7, axis=1) * U[...]
            GB[j] = (h * GF[j]).astype(BF16)
            UB[j] = (h * SIL[j]).astype(BF16)
        g = jnp.concatenate([GB[j] for j in js], axis=0)
        u = jnp.concatenate([UB[j] for j in js], axis=0)
        part = dot(g, GWT[...]) + dot(u, UWT[...])
        for i, j in enumerate(js):
            mine = part[48 * i : 48 * (i + 1)]
            CS[j] = mine.astype(BF16)

            @pl.when(j == col)
            def _():
                OWN[...] = mine

            @pl.when(j != col)
            def _():
                remote(CS.at[j], RIN.at[col], "cs", "cs", (row, j)).start()

    tokens("s0", 0)
    tokens("s2", -2, 2)
    tokens("s1", -1, 1)
    came("h3", HA.at[0:2])
    h_forward("s3", -3, 3)
    came("h4", HA.at[0])
    h_forward("s4", 4)
    tokens("s3", -3, 3)
    tokens("s4", 4)

    came("no", NO.at[0:12])
    NOT[...] = NO[...].reshape(768, 256).T
    o_gate[...] = dot(NOT[...], GB[...].reshape(768, 896)).astype(BF16)
    s_gate = load(o_gate, o_gate_h)
    o_up[...] = dot(NOT[...], UB[...].reshape(768, 896)).astype(BF16)
    s_up = load(o_up, o_up_h)
    o_down[...] = dot_tn(ACT[...].reshape(768, 896), OG[...].reshape(768, 256)).astype(BF16)
    s_down = load(o_down, o_down_h)

    left("go", GO.at[0:15])
    left("no", NO.at[0:15])
    left("vg", VG.at[0:15])
    left("guz", GU.at[0, 0:7, 0])
    left("guy", GU.at[0, :, 0])
    left("gus", GU.at[0])
    left("pk", PK)
    left("rs", SB.at[0:7])
    left("y", YS)
    left("ha", HA.at[0:7])
    left("has", HA.at[0:8])
    left("m0", M0)
    left("m1", M1)
    left("m2", MZ)

    remote(RIN.at[0:15], RIN.at[0:15], "cs", "cs", sib).wait()
    total = OWN[...]
    for i in range(1, 16):
        total = total + RIN[(col + i) % 16].astype(F32)
    o_normed[...] = total.astype(BF16)
    s_normed = load(o_normed, o_normed_h)
    for cp in (s_gate, s_up, s_down, s_normed):
        cp.wait()

def per_device(normed, gate_w, up_w, down_w, gate_pre, up_pre, block_out, value_w, q_target, grad_out):
    hbm = pl.BlockSpec(memory_space=pltpu.HBM)
    vmem = pl.BlockSpec(memory_space=pltpu.VMEM)
    scratch = [
        pltpu.VMEM((16, 48, 256), BF16),
        pltpu.VMEM((16, 48, 256), BF16),
        pltpu.VMEM((2, 8, 2, 48, 896), BF16),
        pltpu.VMEM((256, 896), BF16),
        pltpu.VMEM((256, 896), BF16),
        pltpu.VMEM((896, 256), BF16),
        pltpu.VMEM((896, 256), BF16),
        pltpu.VMEM((896, 256), BF16),
        pltpu.VMEM((256, 768), BF16),
        pltpu.VMEM((8, 48, 896), BF16),
        pltpu.VMEM((8, 48, 896), BF16),
        pltpu.VMEM((8, 48, 896), F32),
        pltpu.VMEM((8, 48, 896), BF16),
        pltpu.VMEM((48, 896), BF16),
        pltpu.VMEM((48, 896), BF16),
        pltpu.VMEM((48, 896), BF16),
        pltpu.VMEM((48, 896), BF16),
        pltpu.VMEM((4, 48, 896), BF16),
        pltpu.VMEM((48, 896), F32),
        pltpu.VMEM((48, 896), BF16),
        pltpu.VMEM((48, 896), BF16),
        pltpu.VMEM((16, 48, 896), BF16),
        pltpu.VMEM((16, 48, 896), F32),
        pltpu.VMEM((16, 48, 896), F32),
        pltpu.VMEM((16, 48, 896), BF16),
        pltpu.VMEM((16, 48, 896), BF16),
        pltpu.VMEM((16, 48, 896), BF16),
        pltpu.VMEM((16, 48, 256), BF16),
        pltpu.VMEM((16, 48, 256), BF16),
        pltpu.VMEM((16, 48, 256), BF16),
        pltpu.VMEM((48, 256), F32),
        pltpu.VMEM((48, 256), BF16),
        pltpu.VMEM((256, 896), BF16),
        pltpu.VMEM((256, 896), BF16),
        pltpu.VMEM((896, 256), BF16),
        pltpu.VMEM((8, 128), F32),
        pltpu.VMEM((8, 128), F32),
        pltpu.VMEM((8, 128), F32),
        pltpu.VMEM((8, 128), F32),
        pltpu.VMEM((8, 128), F32),
        pltpu.VMEM((7, 8, 128), F32),
        pltpu.VMEM((16, 8, 128), F32),
        pltpu.VMEM((16, 48, 128), F32),
        pltpu.VMEM((1, 896), F32),
        pltpu.SemaphoreType.DMA((N_LOCAL,)),
        pltpu.SemaphoreType.DMA((N_SEND,)),
        pltpu.SemaphoreType.DMA((N_RECV,)),
    ]
    outs = pl.pallas_call(
        kernel,
        out_shape=(
            jax.ShapeDtypeStruct((48, 256), BF16),
            jax.ShapeDtypeStruct((256, 896), BF16),
            jax.ShapeDtypeStruct((256, 896), BF16),
            jax.ShapeDtypeStruct((896, 256), BF16),
        ),
        in_specs=[hbm, hbm, hbm, hbm, vmem, vmem, vmem, vmem, vmem, hbm],
        out_specs=(hbm, hbm, hbm, hbm),
        scratch_shapes=scratch,
        compiler_params=pltpu.CompilerParams(
            collective_id=0, has_side_effects=True, vmem_limit_bytes=60 * 2**20
        ),
    )(
        normed, gate_w, up_w, down_w, gate_pre, up_pre, block_out,
        value_w.reshape(1, 256), q_target.reshape(1, 48), grad_out,
    )
    return outs

def solution(mesh):
    return jax.shard_map(
        per_device,
        mesh=mesh,
        in_specs=(
            P("col", "row"),
            P("row", "col"),
            P("row", "col"),
            P("col", "row"),
            P("row", "col"),
            P("row", "col"),
            P("col", "row"),
            P("row"),
            P("col"),
            P("col", "row"),
        ),
        out_specs=(P("col", "row"), P("row", "col"), P("row", "col"), P("col", "row")),
        check_vma=False,
    )
```

time: 541 us -> 72.8 us (0.13)
  the two profiles are of different devices: /device:TPU:64 before, /device:TPU:17 now
where the time goes in v2:
time: 72.8 us; the launch traced here: 72.4 us
  Pallas kernels  66.5 us (91%)
  local copies, waits for them, and re-layouts  5.18 us (7%)
    pallas_call x1, Pallas kernels, per_device(): pl.pallas_call(kernel, out_shape=(jax.ShapeDtypeStruct((48, 256), BF16),...  66.5 us
    unnamed x8, local copies, waits for them, and re-layouts  5.18 us

profile of v2, /device:TPU:17, one launch (start us, length us, event | category | flops | bytes accessed | tf_op | source)
XLA Modules:
  0.0 72.4 jit_solution(3805424910624985774)
XLA Ops:
  0.6 66.5 %shard_map.129 = (bf16[48,256]{1,0:T(8,128)(2,1)}, bf16[256,896]{1,0:T(8,128)(2,1)}, bf16[256,896]{1,0:T(8,128)(2,1)}, bf16[896,256]{1,0:T(8,128)(2,1)}) custom-call(bf16[48,256]{1,0:T(8,128)(2,1)} %normed_h.1, bf16[256,896]{1,0:T(8,128)(2,1)} %gate_w_h.1, bf16[256,896]{1,0:T(8,128)(2,1)} %up_w_h.1, bf16[896,256]{1,0:T(8,128)(2,1)} %down_w_h.1, ...), custom_call_target="tpu_custom_call" | custom-call | tf_op jit(solution)/shard_map/pallas_call | solution.py:491
  67.2 1.3 %copy.18 = bf16[48,256]{1,0:T(8,128)(2,1)} copy(bf16[48,256]{1,0:T(8,128)(2,1)} %get-tuple-element.8) | data formatting | bytes 49152
  68.5 0.0 copy-start.1
  68.5 1.9 %copy.19 = bf16[256,896]{1,0:T(8,128)(2,1)} copy(bf16[256,896]{1,0:T(8,128)(2,1)} %get-tuple-element.9) | data formatting | bytes 917504
  70.4 0.0 copy-done.1
  70.4 0.0 copy-start
  70.4 0.8 %copy.20 = bf16[256,896]{1,0:T(8,128)(2,1)} copy(bf16[256,896]{1,0:T(8,128)(2,1)S(1)} %copy-done.1) | data formatting | bytes 917504
  71.2 0.4 copy-done
  71.6 0.8 %copy.21 = bf16[896,256]{1,0:T(8,128)(2,1)} copy(bf16[896,256]{1,0:T(8,128)(2,1)S(1)} %copy-done) | data formatting | bytes 917504
Async XLA Ops:
  68.5 1.9 %copy-start.1 = (bf16[256,896]{1,0:T(8,128)(2,1)S(1)}, bf16[256,896]{1,0:T(8,128)(2,1)}, u32[]{:S(2)}) copy-start(bf16[256,896]{1,0:T(8,128)(2,1)} %get-tuple-element.10) | copy-start | bytes 1376260
  70.4 1.2 %copy-start = (bf16[896,256]{1,0:T(8,128)(2,1)S(1)}, bf16[896,256]{1,0:T(8,128)(2,1)}, u32[]{:S(2)}) copy-start(bf16[896,256]{1,0:T(8,128)(2,1)} %get-tuple-element.11) | copy-start | bytes 1376260

commit v3 on v2

--- a/solution.py
+++ b/solution.py
@@ -14,28 +14,32 @@
 
 PARTS = ((0, 256, 512), (512, 640, 896))
 CUT = 512
-N_SEND = 16
-N_RECV = 56
+VMEM_BYTES = 60 * 2**20
+N_SEND = 17
+N_RECV = 47
 N_LOCAL = 9
-DIRECT = False
 
 NT = (((1,), (1,)), ((), ()))
 TN = (((0,), (0,)), ((), ()))
 
+
 def dot_nt(a, b):
     return lax.dot_general(a, b, NT, preferred_element_type=F32)
 
+
 def dot_tn(a, b):
     return lax.dot_general(a, b, TN, preferred_element_type=F32)
 
+
 def dot(a, b):
     return jnp.dot(a, b, preferred_element_type=F32)
+
 
 def kernel(
     normed_h, gate_w_h, up_w_h, down_w_h, gate_pre, up_pre, block_out, value_w, q_target, grad_out_h,
     o_normed_h, o_gate_h, o_up_h, o_down_h,
-    GO, NO, GU, gw, uw, dw, GWT, UWT, NOT,
-    PK, SIN, PO, SB, RA1, RA2, RB1, RB2, RF, OWNH, YS, YR, HA,
+    GO, GOS, NO, GU, gw, uw, DW, GWT, UWT, NOT,
+    KEEP, SB, RA1, RA2, RB1, RB2, RF, OWNH, YS, YR, HA,
     SIL, GF, ACT, GB, UB, OG,
     CS, RIN, OWN, o_normed, o_gate, o_up, o_down,
     M0, MS, M1, MY, M2, MZ, VG, VC, U,
@@ -64,7 +68,7 @@
     ydev = {d: dev(yh_=yd(d)) for d in (1, 2, 3)}
 
     ids = {"send": {}, "recv": {}}
-    started, arrived, loads = [], set(), []
+    loads = []
 
     def sem(side, name):
         known = ids[side]
@@ -79,13 +83,10 @@
         )
 
     def send(src, dst, group, name, to):
-        cp = remote(src, dst, group, name, to)
-        cp.start()
-        started.append((cp, name))
+        remote(src, dst, group, name, to).start()
 
     def came(name, ref):
         remote(ref, ref, "none", name, sib).wait_recv()
-        arrived.add(name)
 
     def left(group, ref):
         remote(ref, ref, group, "none", sib).wait_send()
@@ -96,24 +97,12 @@
         loads.append(cp)
         return cp
 
-    def finish():
-        for cp in loads:
-            if all(cp is not w for w in waited):
-                cp.wait()
-        for cp, name in started:
-            cp.wait_send()
-            if name not in arrived:
-                cp.wait_recv()
-
-    waited = []
-
     def ready(*cps):
         for cp in cps:
             cp.wait()
-            waited.append(cp)
 
     l_go = load(grad_out_h, GO.at[col])
-    l_dw = load(down_w_h, dw)
+    l_dw = load(down_w_h, DW.at[:, :256])
     l_no = load(normed_h, NO.at[col])
     l_gw = load(gate_w_h, gw)
     l_uw = load(up_w_h, uw)
@@ -133,21 +122,20 @@
 
     def gather_y(buf, group, name):
         for d in (2, 1, 3):
-            send(buf.at[col], buf.at[col], group, name + str(d), ydev[d])
+            send(buf.at[col], buf.at[col], group, name if d == 2 else name + str(d), ydev[d])
+        for d in (2, 1, 3):
+            send(buf.at[col], buf.at[col], group, name, dev(x_=xd(d), yh_=yd(2)))
         for d in (2, 1, 3):
             send(buf.at[col], buf.at[col], group, name, xdev[d])
 
     def gather_x(buf, group, name):
-        for dy in (1, 3, 2):
+        for dy in (1, 3):
             at = yd(-dy) * 4 + x
             came(name + str(dy), buf.at[at])
             for d in (2, 1, 3):
                 send(buf.at[at], buf.at[at], group, name, xdev[d])
 
-    if DIRECT:
-        gather_direct(GO, "go", "go")
-    else:
-        gather_y(GO, "go", "go")
+    gather_y(GO, "go", "go")
 
     def gu(d):
         return GU.at[yl, zd(d), k]
@@ -157,8 +145,7 @@
 
     for d, name in ((2, "gu+2"), (-2, "gu-2"), (1, "gu1"), (-1, "gu1")):
         send(gu(0), gu(0), "guz", name, zdev[d])
-    if not DIRECT:
-        gu_y(0)
+    gu_y(0)
 
     ready(l_dw)
     vw = value_w[...]
@@ -166,7 +153,8 @@
     mid = (vw - hi).astype(BF16).astype(F32)
     lo = vw - hi - mid
     terms = jnp.concatenate([hi, mid, lo, jnp.zeros((5, 256), F32)], axis=0).astype(BF16)
-    u_part = jnp.sum(dot_nt(terms, dw[...]), axis=0, keepdims=True)
+    send(DW.at[:, :256], DW.at[:, 256:], "dw", "dw", sib)
+    u_part = jnp.sum(dot_nt(terms, DW[:, :256]), axis=0, keepdims=True)
     v_part = jnp.sum(dot_nt(terms, block_out[...]), axis=0, keepdims=True)
     M0[...] = jnp.zeros((8, 128), F32)
     for i in range(7):
@@ -174,8 +162,7 @@
     M0[7:8, 0:48] = v_part
     send(M0, MS, "m0", "m0", sib)
 
-    if not DIRECT:
-        gather_x(GO, "go", "go")
+    gather_x(GO, "go", "go")
 
     came("m0", MS)
     M1[...] = M0[...] + MS[...]
@@ -193,46 +180,29 @@
     for i, d in enumerate((4, 3, -3, 2, -2, 1, -1)):
         send(M2, MZ.at[i], "m2", "m2", zdev[d])
 
-    if not DIRECT:
-        gu_y(-2)
-        gu_y(2)
-        came("gu1", GU.at[0, 0:2, 0])
-        gu_y(-1)
-        gu_y(1)
-
-    if DIRECT:
-        came("go", GO.at[0:15])
-    else:
-        came("go", GO.at[0:12])
-
-    order = (3, -3, 4, 2, -2, 1, -1, 0)
-    slot = {d: i for i, d in enumerate(order)}
-    pairs = ((3, -3), (4, 2), (-2, 1), (-1, 0))
-    for h, (lo, _, up) in enumerate(PARTS):
-        for i, (d0, d1) in enumerate(pairs):
-            a = jnp.concatenate([GO[(1 - k) * 8 + zd(d0)], GO[(1 - k) * 8 + zd(d1)]], axis=0)
-            p = dot_nt(a, dw[lo:up]).astype(BF16)
-            PK[2 * i, :, lo:up] = p[:48]
-            PK[2 * i + 1, :, lo:up] = p[48:]
-            at = pl.ds(2 * i, 2)
-            send(PK.at[at, :, lo:up], SIN.at[at, :, lo:up], "pk", ("sin", i, h), sib)
-        for i, (d0, d1) in enumerate(pairs):
-            a = jnp.concatenate([GO[k * 8 + zd(d0)], GO[k * 8 + zd(d1)]], axis=0)
-            p = dot_nt(a, dw[lo:up])
-            PO[2 * i, :, lo:up] = p[:48]
-            PO[2 * i + 1, :, lo:up] = p[48:]
-
-    def pair_sum(d, h):
+    gu_y(-2)
+    gu_y(2)
+    came("go", GO.at[0:13])
+
+    half = pl.ds((1 - k) * 8, 8)
+    send(GO.at[half], GOS, "gos", "gos", sib)
+    came("dw", DW.at[:, 256:])
+    came("gos", GOS)
+    slot = {d: i for i, d in enumerate((3, -3, 4, 2, -2, 1, -1))}
+
+    def partial(ds, h):
         lo, _, up = PARTS[h]
-        i = slot[d] // 2
-        if ("sin", i, h) not in arrived:
-            came(("sin", i, h), SIN.at[pl.ds(2 * i, 2), :, lo:up])
-        return PO[slot[d], :, lo:up] + SIN[slot[d], :, lo:up].astype(F32)
+        rows = [jnp.concatenate([GO[k * 8 + zd(d)], GOS[zd(d)]], axis=1) for d in ds]
+        p = dot_nt(jnp.concatenate(rows, axis=0), DW[lo:up])
+        return [p[48 * i : 48 * (i + 1)] for i in range(len(ds))]
 
     def rs_first(h):
         lo, cut, up = PARTS[h]
-        for d in (3, -3, 4):
-            SB[slot[d], :, lo:up] = pair_sum(d, h).astype(BF16)
+        for d, p in zip((3, -3, 4, 2), partial((3, -3, 4, 2), h)):
+            if d == 2:
+                KEEP[1, :, lo:up] = p
+                continue
+            SB[slot[d], :, lo:up] = p.astype(BF16)
             src = SB.at[slot[d]]
             if d == 3:
                 send(src.at[:, lo:up], RA1.at[:, lo:up], "rs", ("a1", h), zdev[1])
@@ -244,20 +214,23 @@
 
     def rs_near(h):
         lo, cut, up = PARTS[h]
+        p = partial((1, -1, -2, 0), h)
         for i, d in enumerate((1, -1)):
-            SB[slot[d], :, lo:up] = pair_sum(d, h).astype(BF16)
+            SB[slot[d], :, lo:up] = p[i].astype(BF16)
             send(SB.at[slot[d], :, lo:up], RF.at[i, :, lo:up], "rs", ("rf", h), zdev[d])
+        KEEP[2, :, lo:up] = p[2]
+        KEEP[0, :, lo:up] = p[3]
 
     def rs_second(h):
         lo, cut, up = PARTS[h]
-        t = pair_sum(2, h)
+        t = KEEP[1, :, lo:up]
         came(("a1", h), RA1.at[:, lo:up])
         came(("a2", h), RA2.at[:, lo:cut])
         t = t + RA1[:, lo:up].astype(F32)
         SB[slot[2], :, lo:cut] = (t[:, : cut - lo] + RA2[:, lo:cut].astype(F32)).astype(BF16)
         SB[slot[2], :, cut:up] = t[:, cut - lo :].astype(BF16)
         send(SB.at[slot[2], :, lo:up], RF.at[2, :, lo:up], "rs", ("rf", h), zdev[2])
-        t = pair_sum(-2, h)
+        t = KEEP[2, :, lo:up]
         came(("b1", h), RB1.at[:, lo:up])
         came(("b2", h), RB2.at[:, cut:up])
         t = t + RB1[:, lo:up].astype(F32)
@@ -268,19 +241,16 @@
     rs_first(0)
     rs_first(1)
     rs_near(0)
+    came("gu1", GU.at[0, 0:2, 0])
+    gu_y(-1)
+    gu_y(1)
     rs_second(0)
     rs_near(1)
     rs_second(1)
-
-    if DIRECT:
-        for d in (0, -2, 2):
-            gu_y(d)
-        came("gu1", GU.at[0, 0:2, 0])
-        gu_y(-1)
-        gu_y(1)
     came("gu3", GU.at[0, 0:3, 0])
     for d in (-3, 3, 4):
         gu_y(d)
+
     send(GU.at[yl, :, k], GU.at[yl, :, k], "gus", "gus1", sib)
     came("m2", MZ)
     total = M2[...]
@@ -293,13 +263,9 @@
     VG[col] = jnp.zeros((8, 128), F32)
     VG[col, 0:1, 0:48] = -2.0 * value_scale * weighting * margin
     gather_direct(VG, "vg", "vg")
-    ready(l_no, l_gw, l_uw)
-    gather_y(NO, "no", "no")
-    GWT[...] = gw[...].T
-    UWT[...] = uw[...].T
 
     for h, (lo, _, up) in enumerate(PARTS):
-        t = pair_sum(0, h)
+        t = KEEP[0, :, lo:up]
         came(("rf", h), RF.at[:, :, lo:up])
         for i in range(4):
             t = t + RF[i, :, lo:up].astype(F32)
@@ -307,7 +273,10 @@
         YS[:, lo:up] = t.astype(BF16)
         send(YS.at[:, lo:up], YR.at[:, lo:up], "y", ("y", h), ylp)
 
-    gather_x(NO, "no", "no")
+    ready(l_no, l_gw, l_uw)
+    gather_y(NO, "no", "no")
+    GWT[...] = gw[...].T
+    UWT[...] = uw[...].T
 
     def h_at(d):
         return k * 8 + zd(d)
@@ -329,6 +298,7 @@
             send(HA.at[h_at(d)], HA.at[h_at(d)], "has", name, sib)
 
     h_forward("s0", 0)
+    gather_x(NO, "no", "no")
 
     came("vg", VG.at[0:15])
 
@@ -338,7 +308,7 @@
         OG[j] = (GO[j].astype(F32) + wide * vw).astype(BF16)
         return carry
 
-    lax.fori_loop(0, 16, out_grad, 0)
+    lax.fori_loop(0, 16, out_grad, 0, unroll=4)
     came("guy", GU.at[1 - yl, :, k])
     send(GU.at[1 - yl, :, k], GU.at[1 - yl, :, k], "gus", "gus2", sib)
 
@@ -396,6 +366,8 @@
     tokens("s0", 0)
     tokens("s2", -2, 2)
     tokens("s1", -1, 1)
+    o_down[...] = dot_tn(ACT[...].reshape(768, 896), OG[...].reshape(768, 256)).astype(BF16)
+    s_down = load(o_down, o_down_h)
     came("h3", HA.at[0:2])
     h_forward("s3", -3, 3)
     came("h4", HA.at[0])
@@ -403,14 +375,12 @@
     tokens("s3", -3, 3)
     tokens("s4", 4)
 
-    came("no", NO.at[0:12])
+    came("no", NO.at[0:13])
     NOT[...] = NO[...].reshape(768, 256).T
     o_gate[...] = dot(NOT[...], GB[...].reshape(768, 896)).astype(BF16)
     s_gate = load(o_gate, o_gate_h)
     o_up[...] = dot(NOT[...], UB[...].reshape(768, 896)).astype(BF16)
     s_up = load(o_up, o_up_h)
-    o_down[...] = dot_tn(ACT[...].reshape(768, 896), OG[...].reshape(768, 256)).astype(BF16)
-    s_down = load(o_down, o_down_h)
 
     left("go", GO.at[0:15])
     left("no", NO.at[0:15])
@@ -418,7 +388,8 @@
     left("guz", GU.at[0, 0:7, 0])
     left("guy", GU.at[0, :, 0])
     left("gus", GU.at[0])
-    left("pk", PK)
+    left("gos", GOS)
+    left("dw", DW.at[:, 256:])
     left("rs", SB.at[0:7])
     left("y", YS)
     left("ha", HA.at[0:7])
@@ -436,22 +407,22 @@
     for cp in (s_gate, s_up, s_down, s_normed):
         cp.wait()
 
+
 def per_device(normed, gate_w, up_w, down_w, gate_pre, up_pre, block_out, value_w, q_target, grad_out):
     hbm = pl.BlockSpec(memory_space=pltpu.HBM)
     vmem = pl.BlockSpec(memory_space=pltpu.VMEM)
     scratch = [
         pltpu.VMEM((16, 48, 256), BF16),
+        pltpu.VMEM((8, 48, 256), BF16),
         pltpu.VMEM((16, 48, 256), BF16),
         pltpu.VMEM((2, 8, 2, 48, 896), BF16),
         pltpu.VMEM((256, 896), BF16),
         pltpu.VMEM((256, 896), BF16),
-        pltpu.VMEM((896, 256), BF16),
+        pltpu.VMEM((896, 512), BF16),
         pltpu.VMEM((896, 256), BF16),
         pltpu.VMEM((896, 256), BF16),
         pltpu.VMEM((256, 768), BF16),
-        pltpu.VMEM((8, 48, 896), BF16),
-        pltpu.VMEM((8, 48, 896), BF16),
-        pltpu.VMEM((8, 48, 896), F32),
+        pltpu.VMEM((3, 48, 896), F32),
         pltpu.VMEM((8, 48, 896), BF16),
         pltpu.VMEM((48, 896), BF16),
         pltpu.VMEM((48, 896), BF16),
@@ -500,13 +471,35 @@
         out_specs=(hbm, hbm, hbm, hbm),
         scratch_shapes=scratch,
         compiler_params=pltpu.CompilerParams(
-            collective_id=0, has_side_effects=True, vmem_limit_bytes=60 * 2**20
+            collective_id=0, has_side_effects=True, vmem_limit_bytes=VMEM_BYTES
         ),
     )(
         normed, gate_w, up_w, down_w, gate_pre, up_pre, block_out,
         value_w.reshape(1, 256), q_target.reshape(1, 48), grad_out,
     )
-    return outs
+    return pl.pallas_call(
+        hand_over,
+        out_shape=tuple(jax.ShapeDtypeStruct(o.shape, o.dtype) for o in outs),
+        in_specs=[hbm] * 4,
+        out_specs=(hbm,) * 4,
+        scratch_shapes=[pltpu.VMEM(o.shape, o.dtype) for o in outs]
+        + [pltpu.SemaphoreType.DMA((4,)), pltpu.SemaphoreType.DMA((4,))],
+        compiler_params=pltpu.CompilerParams(vmem_limit_bytes=VMEM_BYTES),
+    )(*outs)
+
+
+def hand_over(a, b, c, d, oa, ob, oc, od, va, vb, vc, vd, s_in, s_out):
+    four = range(4)
+    ins = [pltpu.make_async_copy((a, b, c, d)[i], (va, vb, vc, vd)[i], s_in.at[i]) for i in four]
+    outs = [pltpu.make_async_copy((va, vb, vc, vd)[i], (oa, ob, oc, od)[i], s_out.at[i]) for i in four]
+    for cp in ins:
+        cp.start()
+    for i in four:
+        ins[i].wait()
+        outs[i].start()
+    for cp in outs:
+        cp.wait()
+
 
 def solution(mesh):
     return jax.shard_map(

time: 72.8 us -> 70.4 us (0.967)
  local copies, waits for them, and re-layouts: 5.18 us -> 0 us
  Pallas kernels: 66.5 us -> 69.5 us
    unnamed x8 -> x0, local copies, waits for them, and re-layouts: 5.18 us -> none
    pallas_call x0 -> x1, Pallas kernels: none -> 2.18 us  [per_device(): pl.pallas_call(hand_over, out_shape=tuple((jax.ShapeDtypeStruct(o.shape,...]
    pallas_call x1, Pallas kernels: 66.5 us -> 67.3 us  [per_device(): pl.pallas_call(kernel, out_shape=(jax.ShapeDtypeStruct((48, 256), BF16),...]
where the time goes in v3:
time: 70.4 us; the launch traced here: 70.1 us
  Pallas kernels  69.5 us (99%)
    pallas_call x1, Pallas kernels, per_device(): pl.pallas_call(kernel, out_shape=(jax.ShapeDtypeStruct((48, 256), BF16),...  67.3 us
    pallas_call x1, Pallas kernels, per_device(): pl.pallas_call(hand_over, out_shape=tuple((jax.ShapeDtypeStruct(o.shape,...  2.18 us

profile of v3, /device:TPU:17, one launch (start us, length us, event | category | flops | bytes accessed | tf_op | source)
XLA Modules:
  0.0 70.1 jit_solution(3276220387469053964)
XLA Ops:
  0.6 67.3 %shard_map.129 = (bf16[48,256]{1,0:T(8,128)(2,1)}, bf16[256,896]{1,0:T(8,128)(2,1)}, bf16[256,896]{1,0:T(8,128)(2,1)}, bf16[896,256]{1,0:T(8,128)(2,1)}) custom-call(bf16[48,256]{1,0:T(8,128)(2,1)} %normed_h.1, bf16[256,896]{1,0:T(8,128)(2,1)} %gate_w_h.1, bf16[256,896]{1,0:T(8,128)(2,1)} %up_w_h.1, bf16[896,256]{1,0:T(8,128)(2,1)} %down_w_h.1, ...), custom_call_target="tpu_custom_call" | custom-call | tf_op jit(solution)/shard_map/pallas_call | solution.py:462
  68.0 2.2 %shard_map.130 = (bf16[48,256]{1,0:T(8,128)(2,1)}, bf16[256,896]{1,0:T(8,128)(2,1)}, bf16[256,896]{1,0:T(8,128)(2,1)}, bf16[896,256]{1,0:T(8,128)(2,1)}) custom-call(bf16[48,256]{1,0:T(8,128)(2,1)} %get-tuple-element.8.a, bf16[256,896]{1,0:T(8,128)(2,1)} %get-tuple-element.9.b, bf16[256,896]{1,0:T(8,128)(2,1)} %get-tuple-element.10.c, ...), custom_call_target="tpu_custom_call" | custom-call | tf_op jit(solution)/shard_map/pallas_call | solution.py:480

commit v4 on v3

--- a/solution.py
+++ b/solution.py
@@ -15,9 +15,9 @@
 PARTS = ((0, 256, 512), (512, 640, 896))
 CUT = 512
 VMEM_BYTES = 60 * 2**20
-N_SEND = 17
-N_RECV = 47
-N_LOCAL = 9
+N_SEND = 18
+N_RECV = 50
+N_LOCAL = 14
 
 NT = (((1,), (1,)), ((), ()))
 TN = (((0,), (0,)), ((), ()))
@@ -36,13 +36,13 @@
 
 
 def kernel(
-    normed_h, gate_w_h, up_w_h, down_w_h, gate_pre, up_pre, block_out, value_w, q_target, grad_out_h,
+    normed_h, gate_w_h, up_w_h, down_w_h, gate_pre_h, up_pre_h, block_out_h, value_w_h, q_target_h, grad_out_h,
     o_normed_h, o_gate_h, o_up_h, o_down_h,
-    GO, GOS, NO, GU, gw, uw, DW, GWT, UWT, NOT,
+    GO, GOS, NO, GU, gw, uw, DW, DWT, GWT, UWT, NOT,
     KEEP, SB, RA1, RA2, RB1, RB2, RF, OWNH, YS, YR, HA,
     SIL, GF, ACT, GB, UB, OG,
     CS, RIN, OWN, o_normed, o_gate, o_up, o_down,
-    M0, MS, M1, MY, M2, MZ, VG, VC, U,
+    gate_pre, up_pre, block_out, value_w, q_target, M0, MS, M1, MY, M2, MZ, VG, VC, U,
     local, ss, rs,
 ):
     row, col = lax.axis_index("row"), lax.axis_index("col")
@@ -101,19 +101,20 @@
         for cp in cps:
             cp.wait()
 
+    barrier = pltpu.get_barrier_semaphore()
+    partners = [sib, ylp, *zdev.values()] + [(row, (col + i) % 16) for i in range(1, 16)]
+    for p in partners:
+        pl.semaphore_signal(barrier, inc=1, device_id=p, device_id_type=MESH)
+
     l_go = load(grad_out_h, GO.at[col])
+    l_gu = load(gate_pre_h, gate_pre), load(up_pre_h, up_pre)
+    l_v = load(block_out_h, block_out), load(value_w_h, value_w), load(q_target_h, q_target)
     l_dw = load(down_w_h, DW.at[:, :256])
     l_no = load(normed_h, NO.at[col])
     l_gw = load(gate_w_h, gw)
     l_uw = load(up_w_h, uw)
-
-    barrier = pltpu.get_barrier_semaphore()
-    partners = [sib, ylp, *zdev.values()] + [(row, (col + i) % 16) for i in range(1, 16)]
-    for p in partners:
-        pl.semaphore_signal(barrier, inc=1, device_id=p, device_id_type=MESH)
-
+    ready(l_go, *l_gu)
     GU[yl, z, k] = jnp.concatenate([gate_pre[...].astype(F32), up_pre[...].astype(F32)], axis=0).astype(BF16)
-    ready(l_go)
     pl.semaphore_wait(barrier, len(partners))
 
     def gather_direct(buf, group, name):
@@ -122,14 +123,12 @@
 
     def gather_y(buf, group, name):
         for d in (2, 1, 3):
-            send(buf.at[col], buf.at[col], group, name if d == 2 else name + str(d), ydev[d])
-        for d in (2, 1, 3):
-            send(buf.at[col], buf.at[col], group, name, dev(x_=xd(d), yh_=yd(2)))
+            send(buf.at[col], buf.at[col], group, name + str(d), ydev[d])
         for d in (2, 1, 3):
             send(buf.at[col], buf.at[col], group, name, xdev[d])
 
     def gather_x(buf, group, name):
-        for dy in (1, 3):
+        for dy in (1, 3, 2):
             at = yd(-dy) * 4 + x
             came(name + str(dy), buf.at[at])
             for d in (2, 1, 3):
@@ -141,13 +140,13 @@
         return GU.at[yl, zd(d), k]
 
     def gu_y(d):
-        send(gu(d), gu(d), "guy", "guy", ylp)
+        send(gu(d), gu(d), "guy", "guy" if d else "gp0", ylp)
 
     for d, name in ((2, "gu+2"), (-2, "gu-2"), (1, "gu1"), (-1, "gu1")):
         send(gu(0), gu(0), "guz", name, zdev[d])
     gu_y(0)
 
-    ready(l_dw)
+    ready(l_dw, *l_v)
     vw = value_w[...]
     hi = vw.astype(BF16).astype(F32)
     mid = (vw - hi).astype(BF16).astype(F32)
@@ -168,6 +167,10 @@
     M1[...] = M0[...] + MS[...]
     send(M1, MY, "m1", "m1", ylp)
 
+    pair = GU.at[1 - yl, z, k]
+    came("gp0", pair)
+    for d in (1, -1):
+        send(pair, pair, "gp", "gp1", zdev[d])
     came("gu+2", gu(-2))
     send(gu(-2), gu(-2), "guz", "gu3", zdev[1])
     send(gu(-2).at[:, :CUT], gu(-2).at[:, :CUT], "guz", "gu3", zdev[2])
@@ -182,18 +185,19 @@
 
     gu_y(-2)
     gu_y(2)
-    came("go", GO.at[0:13])
+    came("dw", DW.at[:, 256:])
+    DWT[...] = DW[...].T
+    came("go", GO.at[0:12])
 
     half = pl.ds((1 - k) * 8, 8)
     send(GO.at[half], GOS, "gos", "gos", sib)
-    came("dw", DW.at[:, 256:])
     came("gos", GOS)
     slot = {d: i for i, d in enumerate((3, -3, 4, 2, -2, 1, -1))}
 
     def partial(ds, h):
         lo, _, up = PARTS[h]
         rows = [jnp.concatenate([GO[k * 8 + zd(d)], GOS[zd(d)]], axis=1) for d in ds]
-        p = dot_nt(jnp.concatenate(rows, axis=0), DW[lo:up])
+        p = dot(jnp.concatenate(rows, axis=0), DWT[:, lo:up])
         return [p[48 * i : 48 * (i + 1)] for i in range(len(ds))]
 
     def rs_first(h):
@@ -241,17 +245,6 @@
     rs_first(0)
     rs_first(1)
     rs_near(0)
-    came("gu1", GU.at[0, 0:2, 0])
-    gu_y(-1)
-    gu_y(1)
-    rs_second(0)
-    rs_near(1)
-    rs_second(1)
-    came("gu3", GU.at[0, 0:3, 0])
-    for d in (-3, 3, 4):
-        gu_y(d)
-
-    send(GU.at[yl, :, k], GU.at[yl, :, k], "gus", "gus1", sib)
     came("m2", MZ)
     total = M2[...]
     for i in range(7):
@@ -263,7 +256,15 @@
     VG[col] = jnp.zeros((8, 128), F32)
     VG[col, 0:1, 0:48] = -2.0 * value_scale * weighting * margin
     gather_direct(VG, "vg", "vg")
-
+    rs_second(0)
+    rs_near(1)
+    rs_second(1)
+    came("gu1", GU.at[0, 0:2, 0])
+    came("gu3", GU.at[0, 0:3, 0])
+    for d in (-3, 3, 4):
+        gu_y(d)
+
+    send(GU.at[yl, :, k], GU.at[yl, :, k], "gus", "gus1", sib)
     for h, (lo, _, up) in enumerate(PARTS):
         t = KEEP[0, :, lo:up]
         came(("rf", h), RF.at[:, :, lo:up])
@@ -274,9 +275,13 @@
         send(YS.at[:, lo:up], YR.at[:, lo:up], "y", ("y", h), ylp)
 
     ready(l_no, l_gw, l_uw)
-    gather_y(NO, "no", "no")
     GWT[...] = gw[...].T
     UWT[...] = uw[...].T
+
+    came("gp1", GU.at[0, 0:2, 0])
+    came("guy", GU.at[0, 0:5, 0])
+    send(GU.at[1 - yl, :, k], GU.at[1 - yl, :, k], "gus", "gus2", sib)
+    gather_y(NO, "no", "no")
 
     def h_at(d):
         return k * 8 + zd(d)
@@ -298,7 +303,6 @@
             send(HA.at[h_at(d)], HA.at[h_at(d)], "has", name, sib)
 
     h_forward("s0", 0)
-    gather_x(NO, "no", "no")
 
     came("vg", VG.at[0:15])
 
@@ -309,19 +313,6 @@
         return carry
 
     lax.fori_loop(0, 16, out_grad, 0, unroll=4)
-    came("guy", GU.at[1 - yl, :, k])
-    send(GU.at[1 - yl, :, k], GU.at[1 - yl, :, k], "gus", "gus2", sib)
-
-    for h, (lo, cut, up) in enumerate(PARTS):
-        came(("h", 2, h), HA.at[h_at(-2), :, lo:up])
-        h_send("h3", h_at(-2), lo, up, zdev[1])
-        h_send("h4", h_at(-2), lo, cut, zdev[2])
-        came(("h", -2, h), HA.at[h_at(2), :, lo:up])
-        h_send("h3", h_at(2), lo, up, zdev[-1])
-        h_send("h4", h_at(2), cut, up, zdev[-2])
-    h_forward("s2", -2, 2)
-    came("h1", HA.at[0:2])
-    h_forward("s1", -1, 1)
 
     came("gus1", GU.at[yl, :, 1 - k])
     came("gus2", GU.at[1 - yl, :, 1 - k])
@@ -340,6 +331,18 @@
 
     lax.fori_loop(0, 16, factors, 0)
 
+    for h, (lo, cut, up) in enumerate(PARTS):
+        came(("h", 2, h), HA.at[h_at(-2), :, lo:up])
+        h_send("h3", h_at(-2), lo, up, zdev[1])
+        h_send("h4", h_at(-2), lo, cut, zdev[2])
+        came(("h", -2, h), HA.at[h_at(2), :, lo:up])
+        h_send("h3", h_at(2), lo, up, zdev[-1])
+        h_send("h4", h_at(2), cut, up, zdev[-2])
+    h_forward("s2", -2, 2)
+    came("h1", HA.at[0:2])
+    h_forward("s1", -1, 1)
+
+    gather_x(NO, "no", "no")
     def tokens(name, *ds):
         if name is not None:
             came(name, HA.at[pl.ds(0, len(ds))])
@@ -375,7 +378,7 @@
     tokens("s3", -3, 3)
     tokens("s4", 4)
 
-    came("no", NO.at[0:13])
+    came("no", NO.at[0:12])
     NOT[...] = NO[...].reshape(768, 256).T
     o_gate[...] = dot(NOT[...], GB[...].reshape(768, 896)).astype(BF16)
     s_gate = load(o_gate, o_gate_h)
@@ -386,7 +389,8 @@
     left("no", NO.at[0:15])
     left("vg", VG.at[0:15])
     left("guz", GU.at[0, 0:7, 0])
-    left("guy", GU.at[0, :, 0])
+    left("gp", GU.at[0, 0:2, 0])
+    left("guy", GU.at[0, 0:6, 0])
     left("gus", GU.at[0])
     left("gos", GOS)
     left("dw", DW.at[:, 256:])
@@ -410,7 +414,6 @@
 
 def per_device(normed, gate_w, up_w, down_w, gate_pre, up_pre, block_out, value_w, q_target, grad_out):
     hbm = pl.BlockSpec(memory_space=pltpu.HBM)
-    vmem = pl.BlockSpec(memory_space=pltpu.VMEM)
     scratch = [
         pltpu.VMEM((16, 48, 256), BF16),
         pltpu.VMEM((8, 48, 256), BF16),
@@ -419,6 +422,7 @@
         pltpu.VMEM((256, 896), BF16),
         pltpu.VMEM((256, 896), BF16),
         pltpu.VMEM((896, 512), BF16),
+        pltpu.VMEM((512, 896), BF16),
         pltpu.VMEM((896, 256), BF16),
         pltpu.VMEM((896, 256), BF16),
         pltpu.VMEM((256, 768), BF16),
@@ -446,6 +450,11 @@
         pltpu.VMEM((256, 896), BF16),
         pltpu.VMEM((256, 896), BF16),
         pltpu.VMEM((896, 256), BF16),
+        pltpu.VMEM((24, 896), BF16),
+        pltpu.VMEM((24, 896), BF16),
+        pltpu.VMEM((48, 256), BF16),
+        pltpu.VMEM((1, 256), F32),
+        pltpu.VMEM((1, 48), F32),
         pltpu.VMEM((8, 128), F32),
         pltpu.VMEM((8, 128), F32),
         pltpu.VMEM((8, 128), F32),
@@ -467,7 +476,7 @@
             jax.ShapeDtypeStruct((256, 896), BF16),
             jax.ShapeDtypeStruct((896, 256), BF16),
         ),
-        in_specs=[hbm, hbm, hbm, hbm, vmem, vmem, vmem, vmem, vmem, hbm],
+        in_specs=[hbm] * 10,
         out_specs=(hbm, hbm, hbm, hbm),
         scratch_shapes=scratch,
         compiler_params=pltpu.CompilerParams(

time: 70.4 us -> 66.8 us (0.949)
  Pallas kernels: 69.5 us -> 66 us
    pallas_call x1, Pallas kernels: 67.3 us -> 63.8 us  [per_device(): pl.pallas_call(kernel, out_shape=(jax.ShapeDtypeStruct((48, 256), BF16),...]
where the time goes in v4:
time: 66.8 us; the launch traced here: 66.6 us
  Pallas kernels  66 us (99%)
    pallas_call x1, Pallas kernels, per_device(): pl.pallas_call(kernel, out_shape=(jax.ShapeDtypeStruct((48, 256), BF16),...  63.8 us
    pallas_call x1, Pallas kernels, per_device(): pl.pallas_call(hand_over, out_shape=tuple((jax.ShapeDtypeStruct(o.shape,...  2.18 us

profile of v4, /device:TPU:17, one launch (start us, length us, event | category | flops | bytes accessed | tf_op | source)
XLA Modules:
  0.0 66.6 jit_solution(3633793925760597605)
XLA Ops:
  0.6 63.8 %shard_map.129 = (bf16[48,256]{1,0:T(8,128)(2,1)}, bf16[256,896]{1,0:T(8,128)(2,1)}, bf16[256,896]{1,0:T(8,128)(2,1)}, bf16[896,256]{1,0:T(8,128)(2,1)}) custom-call(bf16[48,256]{1,0:T(8,128)(2,1)} %normed_h.1, bf16[256,896]{1,0:T(8,128)(2,1)} %gate_w_h.1, bf16[256,896]{1,0:T(8,128)(2,1)} %up_w_h.1, bf16[896,256]{1,0:T(8,128)(2,1)} %down_w_h.1, ...), custom_call_target="tpu_custom_call" | custom-call | tf_op jit(solution)/shard_map/pallas_call | solution.py:471
  64.4 2.2 %shard_map.130 = (bf16[48,256]{1,0:T(8,128)(2,1)}, bf16[256,896]{1,0:T(8,128)(2,1)}, bf16[256,896]{1,0:T(8,128)(2,1)}, bf16[896,256]{1,0:T(8,128)(2,1)}) custom-call(bf16[48,256]{1,0:T(8,128)(2,1)} %get-tuple-element.8.a, bf16[256,896]{1,0:T(8,128)(2,1)} %get-tuple-element.9.b, bf16[256,896]{1,0:T(8,128)(2,1)} %get-tuple-element.10.c, ...), custom_call_target="tpu_custom_call" | custom-call | tf_op jit(solution)/shard_map/pallas_call | solution.py:489

commit v5 on v4

--- a/solution.py
+++ b/solution.py
@@ -12,11 +12,11 @@
 BF16 = jnp.bfloat16
 MESH = pl.DeviceIdType.MESH
 
-PARTS = ((0, 256, 512), (512, 640, 896))
+PARTS = ((0, 128, 256), (256, 384, 512), (512, 640, 896))
 CUT = 512
 VMEM_BYTES = 60 * 2**20
 N_SEND = 18
-N_RECV = 50
+N_RECV = 58
 N_LOCAL = 14
 
 NT = (((1,), (1,)), ((), ()))
@@ -244,6 +244,7 @@
 
     rs_first(0)
     rs_first(1)
+    rs_first(2)
     rs_near(0)
     came("m2", MZ)
     total = M2[...]
@@ -256,14 +257,15 @@
     VG[col] = jnp.zeros((8, 128), F32)
     VG[col, 0:1, 0:48] = -2.0 * value_scale * weighting * margin
     gather_direct(VG, "vg", "vg")
-    rs_second(0)
-    rs_near(1)
-    rs_second(1)
     came("gu1", GU.at[0, 0:2, 0])
     came("gu3", GU.at[0, 0:3, 0])
     for d in (-3, 3, 4):
         gu_y(d)
-
+    rs_second(0)
+    rs_near(1)
+    rs_second(1)
+    rs_near(2)
+    rs_second(2)
     send(GU.at[yl, :, k], GU.at[yl, :, k], "gus", "gus1", sib)
     for h, (lo, _, up) in enumerate(PARTS):
         t = KEEP[0, :, lo:up]
@@ -343,10 +345,8 @@
     h_forward("s1", -1, 1)
 
     gather_x(NO, "no", "no")
-    def tokens(name, *ds):
-        if name is not None:
-            came(name, HA.at[pl.ds(0, len(ds))])
-        js = [j for d in ds for j in (k * 8 + zd(d), (1 - k) * 8 + zd(d))]
+    def tokens(kk, *ds):
+        js = [kk * 8 + zd(d) for d in ds]
         for j in js:
             h = HA[j].astype(F32) + jnp.concatenate([VC[j]] * 7, axis=1) * U[...]
             GB[j] = (h * GF[j]).astype(BF16)
@@ -366,17 +366,22 @@
             def _():
                 remote(CS.at[j], RIN.at[col], "cs", "cs", (row, j)).start()
 
-    tokens("s0", 0)
-    tokens("s2", -2, 2)
-    tokens("s1", -1, 1)
+    def theirs(name, *ds):
+        came(name, HA.at[pl.ds(0, len(ds))])
+        return ds
+
+    tokens(k, 0, -2, 2)
+    tokens(1 - k, *theirs("s0", 0), *theirs("s2", -2, 2))
+    tokens(k, -1, 1)
+    tokens(1 - k, *theirs("s1", -1, 1))
     o_down[...] = dot_tn(ACT[...].reshape(768, 896), OG[...].reshape(768, 256)).astype(BF16)
     s_down = load(o_down, o_down_h)
     came("h3", HA.at[0:2])
     h_forward("s3", -3, 3)
     came("h4", HA.at[0])
     h_forward("s4", 4)
-    tokens("s3", -3, 3)
-    tokens("s4", 4)
+    tokens(k, -3, 3, 4)
+    tokens(1 - k, *theirs("s3", -3, 3), *theirs("s4", 4))
 
     came("no", NO.at[0:12])
     NOT[...] = NO[...].reshape(768, 256).T

time: 66.8 us -> 64.9 us (0.972)
  Pallas kernels: 66 us -> 64.1 us
    pallas_call x1, Pallas kernels: 63.8 us -> 61.9 us  [per_device(): pl.pallas_call(kernel, out_shape=(jax.ShapeDtypeStruct((48, 256), BF16),...]
where the time goes in v5:
time: 64.9 us; the launch traced here: 64.8 us
  Pallas kernels  64.1 us (99%)
    pallas_call x1, Pallas kernels, per_device(): pl.pallas_call(kernel, out_shape=(jax.ShapeDtypeStruct((48, 256), BF16),...  61.9 us
    pallas_call x1, Pallas kernels, per_device(): pl.pallas_call(hand_over, out_shape=tuple((jax.ShapeDtypeStruct(o.shape,...  2.18 us

profile of v5, /device:TPU:17, one launch (start us, length us, event | category | flops | bytes accessed | tf_op | source)
XLA Modules:
  0.0 64.8 jit_solution(5821945474732347997)
XLA Ops:
  0.6 61.9 %shard_map.129 = (bf16[48,256]{1,0:T(8,128)(2,1)}, bf16[256,896]{1,0:T(8,128)(2,1)}, bf16[256,896]{1,0:T(8,128)(2,1)}, bf16[896,256]{1,0:T(8,128)(2,1)}) custom-call(bf16[48,256]{1,0:T(8,128)(2,1)} %normed_h.1, bf16[256,896]{1,0:T(8,128)(2,1)} %gate_w_h.1, bf16[256,896]{1,0:T(8,128)(2,1)} %up_w_h.1, bf16[896,256]{1,0:T(8,128)(2,1)} %down_w_h.1, ...), custom_call_target="tpu_custom_call" | custom-call | tf_op jit(solution)/shard_map/pallas_call | solution.py:476
  62.6 2.2 %shard_map.130 = (bf16[48,256]{1,0:T(8,128)(2,1)}, bf16[256,896]{1,0:T(8,128)(2,1)}, bf16[256,896]{1,0:T(8,128)(2,1)}, bf16[896,256]{1,0:T(8,128)(2,1)}) custom-call(bf16[48,256]{1,0:T(8,128)(2,1)} %get-tuple-element.8.a, bf16[256,896]{1,0:T(8,128)(2,1)} %get-tuple-element.9.b, bf16[256,896]{1,0:T(8,128)(2,1)} %get-tuple-element.10.c, ...), custom_call_target="tpu_custom_call" | custom-call | tf_op jit(solution)/shard_map/pallas_call | solution.py:494

commit v6 on v5

--- a/solution.py
+++ b/solution.py
@@ -202,7 +202,7 @@
 
     def rs_first(h):
         lo, cut, up = PARTS[h]
-        for d, p in zip((3, -3, 4, 2), partial((3, -3, 4, 2), h)):
+        for d, p in zip((4, 3, -3, 2), partial((4, 3, -3, 2), h)):
             if d == 2:
                 KEEP[1, :, lo:up] = p
                 continue
@@ -335,11 +335,11 @@
 
     for h, (lo, cut, up) in enumerate(PARTS):
         came(("h", 2, h), HA.at[h_at(-2), :, lo:up])
+        h_send("h4", h_at(-2), lo, cut, zdev[2])
         h_send("h3", h_at(-2), lo, up, zdev[1])
-        h_send("h4", h_at(-2), lo, cut, zdev[2])
         came(("h", -2, h), HA.at[h_at(2), :, lo:up])
+        h_send("h4", h_at(2), cut, up, zdev[-2])
         h_send("h3", h_at(2), lo, up, zdev[-1])
-        h_send("h4", h_at(2), cut, up, zdev[-2])
     h_forward("s2", -2, 2)
     came("h1", HA.at[0:2])
     h_forward("s1", -1, 1)

time: 64.9 us -> 65.5 us (level)
  no operation moved by 1% of the time
where the time goes in v6:
time: 65.5 us; the launch traced here: 65.4 us
  Pallas kernels  64.7 us (99%)
    pallas_call x1, Pallas kernels, per_device(): pl.pallas_call(kernel, out_shape=(jax.ShapeDtypeStruct((48, 256), BF16),...  62.5 us
    pallas_call x1, Pallas kernels, per_device(): pl.pallas_call(hand_over, out_shape=tuple((jax.ShapeDtypeStruct(o.shape,...  2.18 us

profile of v6, /device:TPU:17, one launch (start us, length us, event | category | flops | bytes accessed | tf_op | source)
XLA Modules:
  0.0 65.4 jit_solution(14182735151021350671)
XLA Ops:
  0.6 62.5 %shard_map.129 = (bf16[48,256]{1,0:T(8,128)(2,1)}, bf16[256,896]{1,0:T(8,128)(2,1)}, bf16[256,896]{1,0:T(8,128)(2,1)}, bf16[896,256]{1,0:T(8,128)(2,1)}) custom-call(bf16[48,256]{1,0:T(8,128)(2,1)} %normed_h.1, bf16[256,896]{1,0:T(8,128)(2,1)} %gate_w_h.1, bf16[256,896]{1,0:T(8,128)(2,1)} %up_w_h.1, bf16[896,256]{1,0:T(8,128)(2,1)} %down_w_h.1, ...), custom_call_target="tpu_custom_call" | custom-call | tf_op jit(solution)/shard_map/pallas_call | solution.py:476
  63.2 2.2 %shard_map.130 = (bf16[48,256]{1,0:T(8,128)(2,1)}, bf16[256,896]{1,0:T(8,128)(2,1)}, bf16[256,896]{1,0:T(8,128)(2,1)}, bf16[896,256]{1,0:T(8,128)(2,1)}) custom-call(bf16[48,256]{1,0:T(8,128)(2,1)} %get-tuple-element.8.a, bf16[256,896]{1,0:T(8,128)(2,1)} %get-tuple-element.9.b, bf16[256,896]{1,0:T(8,128)(2,1)} %get-tuple-element.10.c, ...), custom_call_target="tpu_custom_call" | custom-call | tf_op jit(solution)/shard_map/pallas_call | solution.py:494
